TPU v7x, 128 devices: a whole 4x4x4 slice. The times are simulated.
128 devices in a mesh: seq: 16 (over x, y_hi, core), col: 8 (over y_lo, z).
Axes of the slice: x: 4, y: 4 (y_hi: 2, y_lo: 2; y = y_hi * 2 + y_lo), z: 4, core: 2. Of those that a mesh axis runs over, the one named last changes fastest.
Arguments:
- inputs: bfloat16 [48, 1024, 768], P('seq', 'col'), as said below
- gain_row: float32 [768], replicated, may hold values from 0.25 to 1.75
- w_row_query: bfloat16 [768, 768], replicated, as said below
- w_row_key: bfloat16 [768, 768], replicated, as said below
- w_row_value: bfloat16 [768, 768], replicated, may hold values from -0.3125 to 0.3125
- w_row_out: bfloat16 [768, 768], replicated, may hold values from -0.3125 to 0.3125
- gain_col: float32 [768], replicated, may hold values from 0.25 to 1.75
- w_col_query: bfloat16 [768, 768], replicated, as said below
- w_col_key: bfloat16 [768, 768], replicated, as said below
- w_col_value: bfloat16 [768, 768], replicated, may hold values from -0.21875 to 0.21875
- w_col_out: bfloat16 [768, 768], replicated, may hold values from -0.21875 to 0.21875
- cotangent: bfloat16 [48, 1024, 768], P('seq', 'col'), may hold values from -6 to 6
Outputs:
- output: bfloat16 [48, 1024, 768], P('seq', 'col')
- grad_inputs: bfloat16 [48, 1024, 768], P('seq', 'col')
Inputs may be any that keep to these rules, and one draw needn't show every extreme that they name: `inputs`: embeddings of the alignment. `w_row_query`: a projection matrix of 768 by 768 entries. `w_row_key`: a projection matrix of 768 by 768 entries. `w_col_query`: a projection matrix of 768 by 768 entries. `w_col_key`: a projection matrix of 768 by 768 entries.
All inputs are finite; a program needn't handle non-finite values.
Results may differ from a plain program's by a relative error of at most 0.014.
Values may be sent and summed in bfloat16 or wider, within the bound.
A program may use at most 192 MiB of HBM per device.

v0:
```python
import math

import jax
import jax.numpy as jnp
from jax import lax
from jax.sharding import PartitionSpec as P

D = 768
H = 12
DH = 64


epsilon = 1e-05


def normalize(values, gain):
    center = jnp.mean(values, axis=-1, keepdims=True)
    centred = values - center
    spread = jnp.mean(centred * centred, axis=-1, keepdims=True)
    return centred * lax.rsqrt(spread + epsilon) * gain


def norm_back(values, gain, grad):
    _, pull = jax.vjp(lambda inner: normalize(inner, gain), values.astype(jnp.float32))
    return pull(grad)[0]


def project(values, weight):
    return jnp.einsum("rcd,de->rce", values, weight, preferred_element_type=jnp.float32)


def project_back(values, weight):
    return jnp.einsum("rce,de->rcd", values, weight, preferred_element_type=jnp.float32)


def heads_of(values):
    return values.reshape(values.shape[0], values.shape[1], H, DH)


def softmax_back(weights, grad):
    return weights * (grad - jnp.sum(weights * grad, axis=-1, keepdims=True))


def on_device(
    inputs,
    gain_row,
    w_row_query,
    w_row_key,
    w_row_value,
    w_row_out,
    gain_col,
    w_col_query,
    w_col_key,
    w_col_value,
    w_col_out,
    cotangent,
):
    f32 = jnp.float32
    bf16 = jnp.bfloat16
    rows_dev = inputs.shape[0]
    cols_dev = inputs.shape[1]
    all_rows = rows_dev * lax.axis_size("seq")
    row_scale = 1.0 / math.sqrt(DH * all_rows)
    col_scale = 1.0 / math.sqrt(DH)
    first = normalize(inputs.astype(f32), gain_row).astype(bf16)
    query = (project(first, w_row_query) * row_scale).astype(bf16)
    keys = project(first, w_row_key).astype(bf16)
    values = project(first, w_row_value).astype(bf16)
    query_h = heads_of(query)
    keys_all, values_all = (
        lax.all_gather(keys, "col", axis=1, tiled=True),
        lax.all_gather(values, "col", axis=1, tiled=True),
    )
    keys_h = heads_of(keys_all)
    values_h = heads_of(values_all)
    partial_value = jnp.einsum("rihe,rjhe->hij", query_h, keys_h, preferred_element_type=f32)
    logits = lax.psum(partial_value.astype(jnp.bfloat16), "seq").astype(jnp.float32)
    weights = jax.nn.softmax(logits, axis=-1)
    weights_b = weights.astype(bf16)
    mixed_h = jnp.einsum("hij,rjhe->rihe", weights_b, values_h, preferred_element_type=f32)
    mixed = mixed_h.reshape(rows_dev, cols_dev, D).astype(bf16)
    middle = (inputs.astype(f32) + project(mixed, w_row_out)).astype(bf16)
    second = normalize(middle.astype(f32), gain_col).astype(bf16)
    query2 = (project(second, w_col_query) * col_scale).astype(bf16)
    keys2 = project(second, w_col_key).astype(bf16)
    values2 = project(second, w_col_value).astype(bf16)
    query_c, keys_c, values_c = (
        lax.all_to_all(query2, "seq", split_axis=1, concat_axis=0, tiled=True),
        lax.all_to_all(keys2, "seq", split_axis=1, concat_axis=0, tiled=True),
        lax.all_to_all(values2, "seq", split_axis=1, concat_axis=0, tiled=True),
    )
    query_ch = heads_of(query_c)
    keys_ch = heads_of(keys_c)
    values_ch = heads_of(values_c)
    scores = jnp.einsum("rche,sche->chrs", query_ch, keys_ch, preferred_element_type=f32)
    col_weights = jax.nn.softmax(scores, axis=-1)
    col_b = col_weights.astype(bf16)
    mixed_c = jnp.einsum("chrs,sche->rche", col_b, values_ch, preferred_element_type=f32)
    mixed_c = mixed_c.reshape(all_rows, -1, D).astype(bf16)
    mixed2 = lax.all_to_all(mixed_c, "seq", split_axis=0, concat_axis=1, tiled=True)
    output = (middle.astype(f32) + project(mixed2, w_col_out)).astype(bf16)
    grad_mixed2 = project_back(cotangent, w_col_out).astype(bf16)
    grad_c = heads_of(lax.all_to_all(grad_mixed2, "seq", split_axis=1, concat_axis=0, tiled=True))
    grad_scores = jnp.einsum("rche,sche->chrs", grad_c, values_ch, preferred_element_type=f32)
    grad_values_c = jnp.einsum("chrs,rche->sche", col_b, grad_c, preferred_element_type=f32)
    grad_sb = softmax_back(col_weights, grad_scores).astype(bf16)
    grad_query_c = (
        jnp.einsum("chrs,sche->rche", grad_sb, keys_ch, preferred_element_type=f32) * col_scale
    )
    grad_keys_c = jnp.einsum("chrs,rche->sche", grad_sb, query_ch, preferred_element_type=f32)
    col_shape = (all_rows, grad_c.shape[1], D)
    grad_query2, grad_keys2, grad_values2 = (
        lax.all_to_all(
            grad_query_c.reshape(col_shape).astype(bf16),
            "seq",
            split_axis=0,
            concat_axis=1,
            tiled=True,
        ),
        lax.all_to_all(
            grad_keys_c.reshape(col_shape).astype(bf16),
            "seq",
            split_axis=0,
            concat_axis=1,
            tiled=True,
        ),
        lax.all_to_all(
            grad_values_c.reshape(col_shape).astype(bf16),
            "seq",
            split_axis=0,
            concat_axis=1,
            tiled=True,
        ),
    )
    grad_second = (
        project_back(grad_query2, w_col_query)
        + project_back(grad_keys2, w_col_key)
        + project_back(grad_values2, w_col_value)
    )
    grad_middle = (cotangent.astype(f32) + norm_back(middle, gain_col, grad_second)).astype(bf16)
    grad_mixed = project_back(grad_middle, w_row_out).astype(bf16)
    grad_h = heads_of(grad_mixed)
    grad_partial = jnp.einsum("rihe,rjhe->hij", grad_h, values_h, preferred_element_type=f32)
    grad_logits = lax.psum(grad_partial.astype(jnp.bfloat16), "seq").astype(jnp.float32)
    grad_lb = softmax_back(weights, grad_logits).astype(bf16)
    grad_query_h = jnp.einsum("hij,rjhe->rihe", grad_lb, keys_h, preferred_element_type=f32)
    grad_query = (grad_query_h.reshape(rows_dev, cols_dev, D) * row_scale).astype(bf16)
    term_keys = jnp.einsum("hij,rihe->jrhe", grad_lb, query_h, preferred_element_type=f32)
    term_values = jnp.einsum("hij,rihe->jrhe", weights_b, grad_h, preferred_element_type=f32)
    summed = lax.psum_scatter(
        jnp.concatenate(
            [
                term_keys.reshape(cols_dev * lax.axis_size("col"), rows_dev, D),
                term_values.reshape(cols_dev * lax.axis_size("col"), rows_dev, D),
            ],
            axis=2,
        ).astype(jnp.bfloat16),
        "col",
        scatter_dimension=0,
        tiled=True,
    ).astype(jnp.float32)
    summed = jnp.transpose(summed, (1, 0, 2))
    grad_keys = summed[:, :, :D].astype(bf16)
    grad_values = summed[:, :, D:].astype(bf16)
    grad_first = (
        project_back(grad_query, w_row_query)
        + project_back(grad_keys, w_row_key)
        + project_back(grad_values, w_row_value)
    )
    grad_inputs = (grad_middle.astype(f32) + norm_back(inputs, gain_row, grad_first)).astype(bf16)
    return (output, grad_inputs)


def solution(mesh):
    in_specs = (
        P("seq", "col", None),
        P(),
        P(),
        P(),
        P(),
        P(),
        P(),
        P(),
        P(),
        P(),
        P(),
        P("seq", "col", None),
    )
    out_specs = (P("seq", "col", None), P("seq", "col", None))
    return jax.shard_map(
        on_device, mesh=mesh, in_specs=in_specs, out_specs=out_specs, check_vma=False
    )
```

profile of v0, /device:TPU:1, one launch (start us, length us, event | category | flops | bytes accessed | tf_op | source)
XLA Modules:
  0.0 756.6 jit_solution(12040563334638527860)
XLA Ops:
  17.4 57.1 %all-gather.5.cloned.1.call-done = bf16[3,1024,768]{2,1,0:T(8,128)(2,1)} async-done(((bf16[3,128,768]{2,1,0:T(8,128)(2,1)}), bf16[3,1024,768]{2,1,0:T(8,128)(2,1)}) %all-gather.5.cloned.1.call-update) | async-done | bytes 4718608 | tf_op jit(solution)/shard_map/all_gather | solution.py:71
  74.5 6.6 copy.68
  81.1 5.0 bitcast_convert_fusion.1
  89.6 7.1 all-to-all-start.4
  96.7 44.8 %all-gather.3.cloned.1.call-done = bf16[3,1024,768]{2,1,0:T(8,128)(2,1)} async-done(((bf16[3,128,768]{2,1,0:T(8,128)(2,1)}), bf16[3,1024,768]{2,1,0:T(8,128)(2,1)}) %all-gather.3.cloned.1.call-update) | async-done | bytes 4718608 | tf_op jit(solution)/shard_map/all_gather | solution.py:72
  141.5 6.6 copy.66
  148.1 141.6 %all-reduce.3.cloned.1.call-done = bf16[12,128,1024]{2,1,0:T(8,128)(2,1)} async-done(((bf16[12,128,1024]{2,1,0:T(8,128)(2,1)}), bf16[12,128,1024]{2,1,0:T(8,128)(2,1)}) %all-reduce.3.cloned.1.call-update) | async-done | bytes 3145744 | tf_op jit(solution)/shard_map/psum | solution.py:77
  295.5 4.1 fusion.61
  304.3 7.8 %all-to-all-start.2 = ((bf16[3,128,768]{2,0,1:T(4,128)(2,1)}), bf16[3,128,768]{2,0,1:T(4,128)(2,1)}, u32[]{:S(2)}, u32[]{:S(2)}) async-start(bf16[3,128,768]{2,0,1:T(4,128)(2,1)} %copy.76), calls=%async_computation.2 | async-start | bytes 1572864 | tf_op jit(solution)/shard_map/all_to_all | solution.py:89
  315.4 10.8 %all-to-all-done.2 = bf16[3,128,768]{2,0,1:T(4,128)(2,1)} async-done(((bf16[3,128,768]{2,0,1:T(4,128)(2,1)}), bf16[3,128,768]{2,0,1:T(4,128)(2,1)}, u32[]{:S(2)}, u32[]{:S(2)}) %all-to-all-start.2) | async-done | bytes 589856 | tf_op jit(solution)/shard_map/all_to_all | solution.py:89
  326.2 5.1 all-to-all-start.1
  333.4 12.2 %all-to-all-done.1 = bf16[3,128,768]{2,0,1:T(4,128)(2,1)} async-done(((bf16[3,128,768]{2,0,1:T(4,128)(2,1)}), bf16[3,128,768]{2,0,1:T(4,128)(2,1)}, u32[]{:S(2)}, u32[]{:S(2)}) %all-to-all-start.1) | async-done | bytes 589856 | tf_op jit(solution)/shard_map/all_to_all | solution.py:88
  345.7 5.1 all-to-all-start
  356.9 8.3 %all-to-all-done = bf16[3,128,768]{2,0,1:T(4,128)(2,1)} async-done(((bf16[3,128,768]{2,0,1:T(4,128)(2,1)}), bf16[3,128,768]{2,0,1:T(4,128)(2,1)}, u32[]{:S(2)}, u32[]{:S(2)}) %all-to-all-start) | async-done | bytes 589856 | tf_op jit(solution)/shard_map/all_to_all | solution.py:90
  373.7 5.1 fusion.138
  378.8 4.4 multiply_reduce_fusion
  390.5 5.4 all-to-all-start.5
  402.9 4.7 all-to-all-done.5
  407.6 4.9 all-to-all-start.6
  420.1 4.1 all-to-all-done.6
  424.2 5.5 all-to-all-start.7
  433.8 7.8 %all-to-all-done.7 = bf16[48,8,768]{2,1,0:T(8,128)(2,1)} async-done(((bf16[48,8,768]{2,1,0:T(8,128)(2,1)}), bf16[48,8,768]{2,1,0:T(8,128)(2,1)}, u32[]{:S(2)}, u32[]{:S(2)}) %all-to-all-start.7) | async-done | bytes 589856 | tf_op jit(solution)/shard_map/all_to_all | solution.py:127
  446.7 5.0 bitcast_convert_fusion
  458.7 6.7 copy.107
  465.4 131.8 %all-reduce.5.cloned.1.call-done = bf16[12,128,1024]{2,1,0:T(8,128)(2,1)} async-done(((bf16[12,128,1024]{2,1,0:T(8,128)(2,1)}), bf16[12,128,1024]{2,1,0:T(8,128)(2,1)}) %all-reduce.5.cloned.1.call-update) | async-done | bytes 3145744 | tf_op jit(solution)/shard_map/psum | solution.py:144
  597.2 15.6 %convert_bitcast_fusion.1 = bf16[1024,3,12,64]{0,3,1,2:T(8,128)(2,1)} fusion(bf16[12,128,1024]{2,1,0:T(8,128)(2,1)} %all-reduce.5.cloned.1.call-done, bf16[3,128,12,64]{1,3,2,0:T(8,128)(2,1)S(1)} %bitcast.171, bf16[12,128,1024]{2,1,0:T(8,128)(2,1)} %all-reduce.3.cloned.1.call-done, f32[12,128]{1,0:T(8,128)S(1)} %copy-done.31, f32[12,128]{1,0:T(8,128)S(1)} %reduce_max.24), kind=kOutput, calls=%fused_computation.17 | convolution fusion | flops 625216000 | bytes 11612160 | tf_op jit(solution)/shard_map/hij,rihe->jrhe/dot_general | solution.py:148
  612.8 5.3 copy.103
  618.1 6.6 copy.106
  624.7 9.1 %pad_maximum_fusion = bf16[1024,3,1536]{2,0,1:T(8,128)(2,1)} fusion(bf16[1024,3,768]{2,0,1:T(8,128)(2,1)} %copy.107, bf16[1024,3,768]{2,0,1:T(8,128)(2,1)} %copy.106), kind=kLoop, calls=%fused_computation.2 | loop fusion | flops 18874368 | bytes 18874368 | tf_op jit(solution)/shard_map/concatenate | solution.py:151
  641.7 20.5 %all_to_all.132 = bf16[48,8,768]{2,1,0:T(8,128)(2,1)S(1)} all-to-all(bf16[48,8,768]{2,1,0:T(8,128)(2,1)S(1)} %convert_element_type.160), channel_id=1, replica_groups=mesh['seq'=16,'col'=8] {'seq'}, dimensions={0} | all-to-all | bytes 1179648 | tf_op jit(solution)/shard_map/all_to_all | solution.py:100
  663.7 15.3 %fusion.56 = bf16[3,128,12,64]{1,3,0,2:T(8,128)(2,1)S(1)} fusion(bf16[12,128,1024]{2,1,0:T(8,128)(2,1)} %all-reduce.5.cloned.1.call-done, bf16[3,1024,12,64]{1,3,2,0:T(8,128)(2,1)} %bitcast.166, bf16[12,128,1024]{2,1,0:T(8,128)(2,1)} %all-reduce.3.cloned.1.call-done, f32[12,128]{1,0:T(8,128)S(1)} %copy-done.31, f32[12,128]{1,0:T(8,128)S(1)} %reduce_max.24), kind=kOutput, calls=%fused_computation.75 | convolution fusion | flops 623446528 | bytes 11612160 | tf_op jit(solution)/shard_map/hij,rjhe->rihe/dot_general | solution.py:146
  680.9 63.7 %reduce-scatter.2.cloned.1.call-done = bf16[128,3,1536]{2,0,1:T(8,128)(2,1)} async-done(((bf16[1024,3,1536]{2,0,1:T(8,128)(2,1)}), bf16[128,3,1536]{2,0,1:T(8,128)(2,1)}) %reduce-scatter.2.cloned.1.call-update) | async-done | bytes 1179664 | tf_op jit(solution)/shard_map/reduce_scatter | solution.py:150
  (150 shorter events, 97.9 us)
Async XLA Ops:
  7.2 324.2 %copy-start = (bf16[768,768]{1,0:T(8,128)(2,1)S(1)}, bf16[768,768]{1,0:T(8,128)(2,1)}, u32[]{:S(2)}) copy-start(bf16[768,768]{1,0:T(8,128)(2,1)} %param.21) | copy-start | bytes 3538948
  7.2 3.4 copy-start.2
  7.2 3.4 copy-start.33
  7.2 67.3 %all-gather.5.cloned.1.call-start = ((), (), s32[]{:S(2)}) async-start(), calls=%async_computation.10 | async-start | bytes 5308416 | tf_op jit(solution)/shard_map/all_gather | solution.py:71
  10.6 5.8 copy-start.26
  13.4 3.0 copy-start.14
  13.4 128.1 %all-gather.3.cloned.1.call-start = ((), (), s32[]{:S(2)}) async-start(), calls=%async_computation.9 | async-start | bytes 5308416 | tf_op jit(solution)/shard_map/all_gather | solution.py:72
  16.3 273.5 %all-reduce.3.cloned.1.call-start = ((), (), s32[]{:S(2)}) async-start(), calls=%async_computation.11 | async-start | bytes 6291456 | tf_op jit(solution)/shard_map/psum | solution.py:77
  17.4 63.7 %copy-start.5 = (bf16[3,128,768]{1,2,0:T(8,128)(2,1)}, bf16[3,128,768]{1,2,0:T(8,128)(2,1)S(1)}, u32[]{:S(2)}) copy-start(bf16[3,128,768]{1,2,0:T(8,128)(2,1)S(1)} %copy.67) | copy-start | bytes 1769476
  89.6 214.7 %all-to-all-start.4 = ((bf16[3,128,768]{2,0,1:T(4,128)(2,1)}), bf16[3,128,768]{2,0,1:T(4,128)(2,1)S(1)}, u32[]{:S(2)}, u32[]{:S(2)}) async-start(bf16[3,128,768]{2,0,1:T(4,128)(2,1)} %copy.84), calls=%async_computation.4 | async-start | bytes 1572864 | tf_op jit(solution)/shard_map/all_to_all | solution.py:103
  292.2 3.3 copy-start.3
  295.5 4.1 copy-start.30
  302.2 29.2 %copy-start.28 = (f32[3,128]{1,0:T(4,128)}, f32[3,128]{1,0:T(4,128)S(1)}, u32[]{:S(2)}) copy-start(f32[3,128]{1,0:T(4,128)S(1)} %fusion.125) | copy-start | bytes 4612
  304.3 21.9 %all-to-all-start.2 = ((bf16[3,128,768]{2,0,1:T(4,128)(2,1)}), bf16[3,128,768]{2,0,1:T(4,128)(2,1)}, u32[]{:S(2)}, u32[]{:S(2)}) async-start(bf16[3,128,768]{2,0,1:T(4,128)(2,1)} %copy.76), calls=%async_computation.2 | async-start | bytes 1572864 | tf_op jit(solution)/shard_map/all_to_all | solution.py:89
  326.2 19.5 %all-to-all-start.1 = ((bf16[3,128,768]{2,0,1:T(4,128)(2,1)}), bf16[3,128,768]{2,0,1:T(4,128)(2,1)}, u32[]{:S(2)}, u32[]{:S(2)}) async-start(bf16[3,128,768]{2,0,1:T(4,128)(2,1)} %copy.74), calls=%async_computation.1 | async-start | bytes 1572864 | tf_op jit(solution)/shard_map/all_to_all | solution.py:88
  345.7 19.5 %all-to-all-start = ((bf16[3,128,768]{2,0,1:T(4,128)(2,1)}), bf16[3,128,768]{2,0,1:T(4,128)(2,1)}, u32[]{:S(2)}, u32[]{:S(2)}) async-start(bf16[3,128,768]{2,0,1:T(4,128)(2,1)} %copy.72), calls=%async_computation | async-start | bytes 1572864 | tf_op jit(solution)/shard_map/all_to_all | solution.py:90
  378.8 4.4 copy-start.19
  378.8 4.5 copy-start.8
  390.5 17.1 %all-to-all-start.5 = ((bf16[48,8,768]{2,1,0:T(8,128)(2,1)}), bf16[48,8,768]{2,1,0:T(8,128)(2,1)}, u32[]{:S(2)}, u32[]{:S(2)}) async-start(bf16[48,8,768]{2,1,0:T(8,128)(2,1)} %convert_element_type.167), calls=%async_computation.5 | async-start | bytes 1179648 | tf_op jit(solution)/shard_map/all_to_all | solution.py:113
  400.0 12.5 %copy-start.20 = (f32[8,12,48]{2,1,0:T(8,128)S(1)}, f32[8,12,48]{2,1,0:T(8,128)}, u32[]{:S(2)}) copy-start(f32[8,12,48]{2,1,0:T(8,128)} %copy-done.19) | copy-start | bytes 55300
  407.6 16.6 %all-to-all-start.6 = ((bf16[48,8,768]{2,1,0:T(8,128)(2,1)}), bf16[48,8,768]{2,1,0:T(8,128)(2,1)S(1)}, u32[]{:S(2)}, u32[]{:S(2)}) async-start(bf16[48,8,768]{2,1,0:T(8,128)(2,1)} %convert_element_type.170), calls=%async_computation.6 | async-start | bytes 1179648 | tf_op jit(solution)/shard_map/all_to_all | solution.py:120
  424.2 7.8 %copy-start.7 = (bf16[48,8,768]{2,1,0:T(8,128)(2,1)}, bf16[48,8,768]{2,1,0:T(8,128)(2,1)S(1)}, u32[]{:S(2)}) copy-start(bf16[48,8,768]{2,1,0:T(8,128)(2,1)S(1)} %all-to-all-done.6) | copy-start | bytes 1769476
  424.2 17.3 %all-to-all-start.7 = ((bf16[48,8,768]{2,1,0:T(8,128)(2,1)}), bf16[48,8,768]{2,1,0:T(8,128)(2,1)}, u32[]{:S(2)}, u32[]{:S(2)}) async-start(bf16[48,8,768]{2,1,0:T(8,128)(2,1)} %convert_element_type.173), calls=%async_computation.7 | async-start | bytes 1179648 | tf_op jit(solution)/shard_map/all_to_all | solution.py:127
  429.7 167.5 %all-reduce.5.cloned.1.call-start = ((), (), s32[]{:S(2)}) async-start(), calls=%async_computation.12 | async-start | bytes 6291456 | tf_op jit(solution)/shard_map/psum | solution.py:144
  429.8 2.2 copy-start.13
  441.6 1.9 copy-start.29
  451.8 292.8 %reduce-scatter.2.cloned.1.call-start = ((), (), s32[]{:S(2)}) async-start(), calls=%async_computation.13 | async-start | bytes 10616832 | tf_op jit(solution)/shard_map/reduce_scatter | solution.py:150
  458.7 138.5 %copy-start.6 = (bf16[3,128,768]{1,2,0:T(8,128)(2,1)S(1)}, bf16[3,128,768]{1,2,0:T(8,128)(2,1)}, u32[]{:S(2)}) copy-start(bf16[3,128,768]{1,2,0:T(8,128)(2,1)} %copy-done.5) | copy-start | bytes 1769476
  641.7 20.5 %copy-start.36 = (bf16[768,768]{1,0:T(8,128)(2,1)S(1)}, bf16[768,768]{1,0:T(8,128)(2,1)}, u32[]{:S(2)}) copy-start(bf16[768,768]{1,0:T(8,128)(2,1)} %param.22) | copy-start | bytes 3538948
  744.6 2.3 copy-start.9
  744.6 2.3 copy-start.16
  744.6 2.3 copy-start.34
  (17 other events, 19.5 us)
Sparse Core Ops, SparseCore 0:
  13.5 60.9 all-gather.4
  76.7 64.7 all-gather.2
  144.0 145.7 all-reduce.2
  451.9 145.2 all-reduce.4
  634.0 110.5 reduce-scatter.1
where the time goes:
time: 767 us; the launch traced here: 757 us
  waiting for transfers between devices  487 us (63%)
  matrix products  90.7 us (12%)
  local copies, waits for them, and re-layouts  80 us (10%)
  starting transfers between devices  41.4 us (5%)
  other arithmetic  22.1 us (3%)
  blocking collectives  20.5 us (3%)
  between operations  14.8 us (2%)
    psum x1, waiting for transfers between devices, on_device(): lax.psum(partial_value.astype(jnp.bfloat16), 'seq').astype(jnp.float32)  142 us
    psum x1, waiting for transfers between devices, on_device(): lax.psum(grad_partial.astype(jnp.bfloat16), 'seq').astype(jnp.float32)  132 us
    reduce_scatter x1, waiting for transfers between devices, on_device(): lax.psum_scatter(jnp.concatenate([term_keys.reshape(cols_dev * lax.axis_s...  63.7 us
    all_gather x1, waiting for transfers between devices, on_device(): lax.all_gather(keys, 'col', axis=1, tiled=True)  57.1 us
    all_gather x1, waiting for transfers between devices, on_device(): lax.all_gather(values, 'col', axis=1, tiled=True)  44.8 us
    all_to_all x1, blocking collectives, on_device(): lax.all_to_all(mixed_c, 'seq', split_axis=0, concat_axis=1, tiled=True)  20.5 us
    dot_general x1, matrix products, on_device(): jnp.einsum('hij,rihe->jrhe', grad_lb, query_h, preferred_element_type=f32)  15.6 us
  transfers between devices with their start and end apart: 12, of which 11 were waited for; matrix products, arithmetic and copies ran while one was open for 14% of the time, Pallas kernels for 0%

commit v1 on v0

v1 whole, which is shorter than its diff:
```python
import functools
import math

import jax
import jax.numpy as jnp
from jax import lax
from jax.experimental import pallas as pl
from jax.experimental.pallas import tpu as pltpu
from jax.sharding import PartitionSpec as P

D = 768
H = 12
DH = 64
G = 4
HG = H // G
R3 = 3
E3 = R3 * DH
CB = 128
COLS = 1024
TILE = (HG, E3, CB)
MESH = pl.DeviceIdType.MESH
VMEM_LIMIT = 56 * 2**20

epsilon = 1e-05
f32 = jnp.float32
bf16 = jnp.bfloat16


def normalize(values, gain):
    center = jnp.mean(values, axis=-1, keepdims=True)
    centred = values - center
    spread = jnp.mean(centred * centred, axis=-1, keepdims=True)
    return centred * lax.rsqrt(spread + epsilon) * gain


def norm_back(values, gain, grad):
    _, pull = jax.vjp(lambda inner: normalize(inner, gain), values.astype(f32))
    return pull(grad)[0]


def softmax_back(weights, grad):
    return weights * (grad - jnp.sum(weights * grad, axis=-1, keepdims=True))


class Place:
    def __init__(self):
        s, q = lax.axis_index("seq"), lax.axis_index("col")
        self.s, self.q = s, q
        self.x, self.yh, self.c = lax.div(s, 4), lax.rem(lax.div(s, 2), 2), lax.rem(s, 2)
        self.yl, self.z = lax.div(q, 4), lax.rem(q, 4)
        self.y = self.yh * 2 + self.yl
        self.block = self.yh * 2 + self.c
        self.zh, self.zl = lax.div(self.z, 2), lax.rem(self.z, 2)
        self.same = self.block == self.z

    def at(self, x=None, yh=None, c=None, yl=None, z=None):
        pick = lambda new, old: old if new is None else new
        x, yh, c = pick(x, self.x), pick(yh, self.yh), pick(c, self.c)
        yl, z = pick(yl, self.yl), pick(z, self.z)
        return {"seq": (x * 2 + yh) * 2 + c, "col": yl * 4 + z}

    def along_x(self, k):
        x = lax.rem(self.x + k, 4)
        return x, self.at(x=x)

    def along_z(self, k):
        z = lax.rem(self.z + k, 4)
        return z, self.at(z=z)

    def along_y(self, k):
        y = lax.rem(self.y + k, 4)
        return y, self.at(yh=lax.div(y, 2), yl=lax.rem(y, 2))

    def along_seq(self, k):
        s = lax.rem(self.s + k, 16)
        return s, {"seq": s, "col": self.q}

    def sibling(self):
        return self.at(c=1 - self.c)

    def owner(self, k):
        s = lax.rem(self.s + k, 16)
        return s, {"seq": s, "col": self.yl * 4 + self.block}

    def holder(self, k):
        x, z = lax.rem(self.x + k // 4, 4), lax.rem(self.z + k % 4, 4)
        return x * 4 + z, self.at(x=x, yh=self.zh, c=self.zl, z=z)


def remote(src, dst, send, recv, device):
    return pltpu.make_async_remote_copy(
        src_ref=src, dst_ref=dst, send_sem=send, recv_sem=recv, device_id=device, device_id_type=MESH
    )


def enter(p):
    barrier = pltpu.get_barrier_semaphore()

    def greet(device):
        pl.semaphore_signal(barrier, inc=1, device_id=device, device_id_type=MESH)

    for k in range(1, 4):
        greet(p.along_z(k)[1])
    for k in (1, 3):
        greet(p.along_y(k)[1])
    for k in range(1, 16):
        greet(p.along_seq(k)[1])
        greet(p.owner(k)[1])
        greet(p.holder(k)[1])

    @pl.when(jnp.logical_not(p.same))
    def _():
        greet(p.owner(0)[1])
        greet(p.holder(0)[1])

    pl.semaphore_wait(barrier, 3 + 2 + 3 * 15 + jnp.where(p.same, 0, 2))


def exchange_seq(p, src, dst, send, recv, loc):
    own = pltpu.make_async_copy(src.at[p.s], dst.at[p.s], loc)
    own.start()
    copies = []
    for k in range(1, 16):
        s, device = p.along_seq(k)
        copy = remote(src.at[s], dst.at[p.s], send.at[k - 1], recv.at[k - 1], device)
        copy.start()
        copies.append(copy)

    def finish():
        own.wait()
        for k, copy in enumerate(copies, 1):
            copy.wait_send()
            s, device = p.along_seq(16 - k)
            remote(src.at[s], dst.at[s], send.at[k - 1], recv.at[k - 1], device).wait_recv()

    return finish


def x_sum(p, L, Rx, send, recv):
    copies = []
    for k in range(1, 4):
        x, device = p.along_x(k)
        copy = remote(L.at[x], Rx.at[k - 1], send.at[k - 1], recv.at[k - 1], device)
        copy.start()
        copies.append(copy)
    return copies


def x_gather(p, W, send, recv):
    copies = []
    for k in range(1, 4):
        _, device = p.along_x(k)
        copy = remote(W.at[p.x], W.at[p.x], send.at[k - 1], recv.at[k - 1], device)
        copy.start()
        copies.append(copy)
    return copies


def x_gather_wait(p, W, send, recv):
    for k in range(1, 4):
        x, device = p.along_x(4 - k)
        remote(W.at[x], W.at[x], send.at[k - 1], recv.at[k - 1], device).wait_recv()


class Gather:
    def __init__(self, p, t, src, B, zs, zr, ys, yr, cs, cr, loc):
        self.p, self.t, self.src, self.B = p, t, src, B
        self.zs, self.zr, self.ys, self.yr, self.cs, self.cr = zs, zr, ys, yr, cs, cr
        self.sent = []
        self.own = pltpu.make_async_copy(src.at[p.z], B.at[p.c, p.y, p.z], loc.at[t])

    def send(self, ref, s, r, i, device):
        copy = remote(ref, ref, s.at[self.t, i], r.at[self.t, i], device)
        copy.start()
        self.sent.append(copy)

    def got(self, ref, s, r, i):
        remote(ref, ref, s.at[self.t, i], r.at[self.t, i], self.p.sibling()).wait_recv()

    def z_start(self):
        p = self.p
        self.own.start()
        for k in range(1, 4):
            z, device = p.along_z(k)
            copy = remote(
                self.src.at[z],
                self.B.at[p.c, p.y, p.z],
                self.zs.at[self.t, k - 1],
                self.zr.at[self.t, k - 1],
                device,
            )
            copy.start()
            self.sent.append(copy)

    def z_wait(self):
        p = self.p
        self.own.wait()
        for k in range(1, 4):
            z, _ = p.along_z(4 - k)
            self.got(self.B.at[p.c, p.y, z], self.zs, self.zr, k - 1)

    def ring_start(self):
        p = self.p
        piece = self.B.at[p.c, p.y]
        self.send(piece, self.ys, self.yr, 0, p.along_y(1)[1])
        self.send(piece, self.ys, self.yr, 1, p.along_y(3)[1])
        self.send(piece, self.cs, self.cr, 0, p.sibling())

    def ring_forward(self):
        p = self.p
        left, right = self.B.at[p.c, p.along_y(3)[0]], self.B.at[p.c, p.along_y(1)[0]]
        self.got(left, self.ys, self.yr, 0)
        self.send(left.at[pl.ds(0, 2)], self.ys, self.yr, 2, p.along_y(1)[1])
        self.send(left, self.cs, self.cr, 1, p.sibling())
        self.got(right, self.ys, self.yr, 1)
        self.send(right.at[pl.ds(2, 2)], self.ys, self.yr, 3, p.along_y(3)[1])
        self.send(right, self.cs, self.cr, 2, p.sibling())

    def ring_finish(self):
        p = self.p
        far = self.B.at[p.c, p.along_y(2)[0]]
        self.got(far.at[pl.ds(0, 2)], self.ys, self.yr, 2)
        self.got(far.at[pl.ds(2, 2)], self.ys, self.yr, 3)
        self.send(far, self.cs, self.cr, 3, p.sibling())

    def core_wait(self):
        p = self.p
        for i, k in enumerate((0, 3, 1, 2)):
            self.got(self.B.at[1 - p.c, p.along_y(k)[0]], self.cs, self.cr, i)

    def end(self):
        for copy in self.sent:
            copy.wait_send()


def column_tile(B, j, h):
    yl, z = j // 4, j % 4
    return jnp.concatenate([B[b % 2, (b // 2) * 2 + yl, z, h] for b in range(4)], axis=0)


def dot(a, b, ca, cb):
    return lax.dot_general(a, b, (((ca,), (cb,)), ((), ())), preferred_element_type=f32)


def forward_kernel(
    q_ref, k_ref, v_ref, inp_ref, cot_ref,
    mix_ref, inpc_ref, cotc_ref, ko_ref, vo_ref, qo_ref, wo_ref, po_ref,
    K, V, Q, L, Rx, W, M,
    zs, zr, ys, yr, cs, cr, loc, qs, qr, xs, xr, gs, gr, ms, mr, ts, tr, outs,
):
    p = Place()
    enter(p)
    keys = Gather(p, 0, k_ref, K, zs, zr, ys, yr, cs, cr, loc)
    vals = Gather(p, 1, v_ref, V, zs, zr, ys, yr, cs, cr, loc)
    keys.z_start()

    def query_copy(k):
        z, _ = p.along_z(k)
        device = p.at(yh=p.zh, c=p.zl, z=z)
        return remote(q_ref.at[z], Q.at[p.block], qs.at[k], qr.at[p.block], device)

    own_query = pltpu.make_async_copy(q_ref.at[p.z], Q.at[p.block], loc.at[2])

    @pl.when(p.same)
    def _():
        own_query.start()

    @pl.when(jnp.logical_not(p.same))
    def _():
        query_copy(0).start()

    for k in range(1, 4):
        query_copy(k).start()
    vals.z_start()

    keys.z_wait()
    keys.ring_start()
    end_inp = exchange_seq(p, inp_ref, inpc_ref, ts.at[0], tr.at[0], loc.at[3])
    end_cot = exchange_seq(p, cot_ref, cotc_ref, ts.at[1], tr.at[1], loc.at[4])
    vals.z_wait()
    keys.ring_forward()
    keys.ring_finish()
    vals.ring_start()
    keys.core_wait()

    @pl.when(p.same)
    def _():
        own_query.wait()

    @pl.when(jnp.logical_not(p.same))
    def _():
        b = p.block
        remote(q_ref.at[0], Q.at[b], qs.at[0], qr.at[b], p.holder(0)[1]).wait_recv()
        query_copy(0).wait_send()

    for k in range(1, 4):
        b = lax.rem(p.block + k, 4)
        remote(q_ref.at[0], Q.at[b], qs.at[k], qr.at[b], p.holder(0)[1]).wait_recv()
        query_copy(k).wait_send()

    def logits_head(h, carry):
        qt = jnp.concatenate([Q[b, h] for b in range(4)], axis=0)
        for j in range(8):
            part = dot(qt, column_tile(K, j, h), 0, 0).astype(bf16)
            L[:, h, :, j * CB : (j + 1) * CB] = part.reshape(4, 32, CB)
        return carry

    lax.fori_loop(0, HG, logits_head, 0)
    sums = x_sum(p, L, Rx, xs, xr)
    out_k = pltpu.make_async_copy(K, ko_ref, outs.at[0])
    out_q = pltpu.make_async_copy(Q, qo_ref, outs.at[1])
    out_k.start()
    out_q.start()
    vals.ring_forward()
    for copy in sums:
        copy.wait()

    def weights_head(h, carry):
        logits = L[p.x, h].astype(f32)
        for k in range(3):
            logits = logits + Rx[k, h].astype(f32)
        top = jnp.max(logits, axis=-1, keepdims=True)
        powers = jnp.exp(logits - top)
        weights = powers / jnp.sum(powers, axis=-1, keepdims=True)
        po_ref[h] = weights
        W[p.x, h] = weights.astype(bf16)
        return carry

    lax.fori_loop(0, HG, weights_head, 0)
    gathers = x_gather(p, W, gs, gr)
    vals.ring_finish()
    vals.core_wait()
    x_gather_wait(p, W, gs, gr)
    out_v = pltpu.make_async_copy(V, vo_ref, outs.at[2])
    out_w = pltpu.make_async_copy(W, wo_ref, outs.at[3])
    out_v.start()
    out_w.start()

    def mixed_head(h, carry):
        w = jnp.concatenate([W[x, h] for x in range(4)], axis=0)
        v = jnp.concatenate([column_tile(V, j, h) for j in range(8)], axis=1)
        mixed = dot(w, v, 1, 1)
        M[:, h] = mixed.reshape(16, 8, 4 * E3).astype(bf16)
        return carry

    lax.fori_loop(0, HG, mixed_head, 0)
    here = p.x * 4 + p.z

    def mixed_copy(k):
        s, device = p.owner(k)
        return remote(M.at[s], mix_ref.at[here], ms.at[k], mr.at[here], device)

    own_mixed = pltpu.make_async_copy(M.at[p.s], mix_ref.at[here], loc.at[5])

    @pl.when(p.same)
    def _():
        own_mixed.start()

    @pl.when(jnp.logical_not(p.same))
    def _():
        mixed_copy(0).start()

    for k in range(1, 16):
        mixed_copy(k).start()

    @pl.when(p.same)
    def _():
        own_mixed.wait()

    @pl.when(jnp.logical_not(p.same))
    def _():
        i, device = p.holder(0)
        remote(M.at[0], mix_ref.at[i], ms.at[0], mr.at[i], device).wait_recv()
        mixed_copy(0).wait_send()

    for k in range(1, 16):
        i, device = p.holder(k)
        remote(M.at[0], mix_ref.at[i], ms.at[k], mr.at[i], device).wait_recv()
        mixed_copy(k).wait_send()
    end_inp()
    end_cot()
    keys.end()
    vals.end()
    for copy in gathers:
        copy.wait_send()
    for copy in (out_k, out_q, out_v, out_w):
        copy.wait()


def add_into(dst, index, other, oindex, z0, z1):
    def step(i, carry):
        z, h = lax.div(i, HG), lax.rem(i, HG)
        a = dst[index + (z + z0, h)].astype(f32) + other[oindex + (z, h)].astype(f32)
        dst[index + (z + z0, h)] = a.astype(bf16)
        return carry

    lax.fori_loop(0, (z1 - z0) * HG, step, 0)


class Scatter:
    def __init__(self, p, t, S, C, far, near, out, cs, cr, ys, yr, zs, zr, loc):
        self.p, self.t, self.S, self.C, self.far, self.near, self.out = p, t, S, C, far, near, out
        self.cs, self.cr, self.ys, self.yr, self.zs, self.zr, self.loc = cs, cr, ys, yr, zs, zr, loc
        self.sent = []

    def send(self, src, dst, s, r, device):
        copy = remote(src, dst, s, r, device)
        copy.start()
        self.sent.append(copy)

    def got(self, dst, s, r):
        remote(dst, dst, s, r, self.p.sibling()).wait_recv()

    def core_start(self):
        p, t = self.p, self.t
        self.send(self.S.at[1 - p.c], self.C, self.cs.at[t], self.cr.at[t], p.sibling())

    def ring_start(self):
        p, t = self.p, self.t
        c, S = p.c, self.S
        self.got(self.C, self.cs.at[t], self.cr.at[t])
        y2, y1, y3 = p.along_y(2)[0], p.along_y(1)[0], p.along_y(3)[0]
        d1, d3 = p.along_y(1)[1], p.along_y(3)[1]
        lo, hi = pl.ds(0, 2), pl.ds(2, 2)
        add_into(S, (c, y2), self.C, (y2,), 0, 4)
        self.send(S.at[c, y2, lo], self.far.at[t, 0], self.ys.at[t, 0], self.yr.at[t, 0], d1)
        self.send(S.at[c, y2, hi], self.far.at[t, 1], self.ys.at[t, 1], self.yr.at[t, 1], d3)
        add_into(S, (c, y1), self.C, (y1,), 0, 4)
        add_into(S, (c, y3), self.C, (y3,), 0, 4)
        self.send(S.at[c, y1, hi], self.near.at[t, 0, hi], self.ys.at[t, 2], self.yr.at[t, 2], d1)
        self.send(S.at[c, y3, lo], self.near.at[t, 1, lo], self.ys.at[t, 3], self.yr.at[t, 3], d3)
        add_into(S, (c, p.y), self.C, (p.y,), 0, 4)

    def ring_forward(self):
        p, t = self.p, self.t
        c, S = p.c, self.S
        y1, y3 = p.along_y(1)[0], p.along_y(3)[0]
        d1, d3 = p.along_y(1)[1], p.along_y(3)[1]
        lo, hi = pl.ds(0, 2), pl.ds(2, 2)
        self.got(self.far.at[t, 0], self.ys.at[t, 0], self.yr.at[t, 0])
        add_into(S, (c, y1), self.far, (t, 0), 0, 2)
        self.send(S.at[c, y1, lo], self.near.at[t, 0, lo], self.ys.at[t, 4], self.yr.at[t, 4], d1)
        self.got(self.far.at[t, 1], self.ys.at[t, 1], self.yr.at[t, 1])
        add_into(S, (c, y3), self.far, (t, 1), 2, 4)
        self.send(S.at[c, y3, hi], self.near.at[t, 1, hi], self.ys.at[t, 5], self.yr.at[t, 5], d3)

    def ring_finish(self):
        p, t = self.p, self.t
        c, S = p.c, self.S
        lo, hi = pl.ds(0, 2), pl.ds(2, 2)
        for i, (n, half) in {2: (0, hi), 3: (1, lo), 4: (0, lo), 5: (1, hi)}.items():
            self.got(self.near.at[t, n, half], self.ys.at[t, i], self.yr.at[t, i])

        def step(i, carry):
            z, h = lax.div(i, HG), lax.rem(i, HG)
            a = S[c, p.y, z, h].astype(f32) + self.near[t, 0, z, h].astype(f32)
            a = a + self.near[t, 1, z, h].astype(f32)
            S[c, p.y, z, h] = a.astype(bf16)
            return carry

        lax.fori_loop(0, 4 * HG, step, 0)
        own = pltpu.make_async_copy(S.at[c, p.y, p.z], self.out.at[p.z], self.loc)
        own.start()
        self.own = own
        for k in range(1, 4):
            z, device = p.along_z(k)
            self.send(
                S.at[c, p.y, z], self.out.at[p.z], self.zs.at[t, k - 1], self.zr.at[t, k - 1], device
            )

    def end(self):
        p, t = self.p, self.t
        self.own.wait()
        for k in range(1, 4):
            z, _ = p.along_z(4 - k)
            self.got(self.out.at[z], self.zs.at[t, k - 1], self.zr.at[t, k - 1])
        for copy in self.sent:
            copy.wait_send()


def backward_kernel(
    row_scale,
    g_ref, k_ref, v_ref, q_ref, w_ref, p_ref, out_ref, mid_ref,
    outr_ref, midr_ref, gq_ref, gk_ref, gv_ref,
    K, V, Q, W, Pw, Gm, L, Rx, Wg, SK, SV, CK, CV, far, near, GQ,
    zs, zr, ys, yr, cs, cr, loc, qs, qr, xs, xr, gs, gr, ms, mr, ts, tr, ins,
):
    p = Place()
    loads = []
    for i, (src, dst) in enumerate(((v_ref, V), (w_ref, W), (k_ref, K), (q_ref, Q), (p_ref, Pw))):
        copy = pltpu.make_async_copy(src, dst, ins.at[i])
        copy.start()
        loads.append(copy)
    enter(p)

    def grad_copy(k):
        i, device = p.holder(k)
        return remote(g_ref.at[i], Gm.at[p.s], ms.at[k], mr.at[p.s], device)

    own_grad = pltpu.make_async_copy(g_ref.at[p.x * 4 + p.z], Gm.at[p.s], loc.at[0])

    @pl.when(p.same)
    def _():
        own_grad.start()

    @pl.when(jnp.logical_not(p.same))
    def _():
        grad_copy(0).start()

    for k in range(1, 16):
        grad_copy(k).start()

    @pl.when(p.same)
    def _():
        own_grad.wait()

    @pl.when(jnp.logical_not(p.same))
    def _():
        s, device = p.owner(0)
        remote(g_ref.at[0], Gm.at[s], ms.at[0], mr.at[s], device).wait_recv()
        grad_copy(0).wait_send()

    for k in range(1, 16):
        s, device = p.owner(k)
        remote(g_ref.at[0], Gm.at[s], ms.at[k], mr.at[s], device).wait_recv()
        grad_copy(k).wait_send()
    for copy in loads:
        copy.wait()

    def grad_of(h):
        return Gm[:, h].astype(f32).reshape(CB, 4 * E3).astype(bf16)

    def logits_head(h, carry):
        g = grad_of(h)
        for j in range(8):
            part = dot(g, column_tile(V, j, h), 1, 0).astype(bf16)
            L[:, h, :, j * CB : (j + 1) * CB] = part.reshape(4, 32, CB)
        return carry

    lax.fori_loop(0, HG, logits_head, 0)
    sums = x_sum(p, L, Rx, xs, xr)

    def spread(S, h, j, tile):
        tile = tile.astype(bf16)
        for b in range(4):
            S[b % 2, (b // 2) * 2 + j // 4, j % 4, h] = tile[b * E3 : (b + 1) * E3]

    def values_head(h, carry):
        gt = grad_of(h)
        w = jnp.concatenate([W[x, h] for x in range(4)], axis=0)
        for j in range(8):
            spread(SV, h, j, dot(gt, w[:, j * CB : (j + 1) * CB], 0, 0))
        return carry

    lax.fori_loop(0, HG, values_head, 0)
    vals = Scatter(p, 0, SV, CV, far, near, gv_ref, cs, cr, ys, yr, zs, zr, loc.at[1])
    keys = Scatter(p, 1, SK, CK, far, near, gk_ref, cs, cr, ys, yr, zs, zr, loc.at[2])
    vals.core_start()
    vals.ring_start()
    for copy in sums:
        copy.wait()

    def weights_head(h, carry):
        grad = L[p.x, h].astype(f32)
        for k in range(3):
            grad = grad + Rx[k, h].astype(f32)
        weights = Pw[h]
        grad = weights * (grad - jnp.sum(weights * grad, axis=-1, keepdims=True))
        Wg[p.x, h] = grad.astype(bf16)
        return carry

    lax.fori_loop(0, HG, weights_head, 0)
    gathers = x_gather(p, Wg, gs, gr)
    end_out = exchange_seq(p, out_ref, outr_ref, ts.at[0], tr.at[0], loc.at[3])
    end_mid = exchange_seq(p, mid_ref, midr_ref, ts.at[1], tr.at[1], loc.at[4])
    vals.ring_forward()
    x_gather_wait(p, Wg, gs, gr)

    def keys_head(h, carry):
        qt = jnp.concatenate([Q[b, h] for b in range(4)], axis=0)
        w = jnp.concatenate([Wg[x, h] for x in range(4)], axis=0)
        for j in range(8):
            spread(SK, h, j, dot(qt, w[:, j * CB : (j + 1) * CB], 1, 0))
        return carry

    lax.fori_loop(0, HG, keys_head, 0)
    keys.core_start()

    def query_head(h, carry):
        w = jnp.concatenate([Wg[x, h] for x in range(4)], axis=0)
        kt = jnp.concatenate([column_tile(K, j, h) for j in range(8)], axis=1)
        gq = (dot(kt, w, 1, 1) * row_scale).astype(bf16)
        for b in range(4):
            GQ[b, h] = gq[b * E3 : (b + 1) * E3]
        return carry

    lax.fori_loop(0, HG, query_head, 0)
    keys.ring_start()

    def query_copy(k):
        b = lax.rem(p.block + k, 4)
        device = p.at(yh=lax.div(b, 2), c=lax.rem(b, 2), z=p.block)
        return remote(GQ.at[b], gq_ref.at[p.z], qs.at[k], qr.at[p.z], device)

    own_query = pltpu.make_async_copy(GQ.at[p.block], gq_ref.at[p.z], loc.at[5])

    @pl.when(p.same)
    def _():
        own_query.start()

    @pl.when(jnp.logical_not(p.same))
    def _():
        query_copy(0).start()

    for k in range(1, 4):
        query_copy(k).start()

    vals.ring_finish()
    keys.ring_forward()
    keys.ring_finish()

    @pl.when(p.same)
    def _():
        own_query.wait()

    @pl.when(jnp.logical_not(p.same))
    def _():
        remote(GQ.at[0], gq_ref.at[p.z], qs.at[0], qr.at[p.z], p.holder(0)[1]).wait_recv()
        query_copy(0).wait_send()

    for k in range(1, 4):
        z, _ = p.along_z(k)
        remote(GQ.at[0], gq_ref.at[z], qs.at[k], qr.at[z], p.holder(0)[1]).wait_recv()
        query_copy(k).wait_send()
    vals.end()
    keys.end()
    end_out()
    end_mid()
    for copy in gathers:
        copy.wait_send()


ANY = pl.BlockSpec(memory_space=pl.ANY)
VM = pl.BlockSpec(memory_space=pltpu.VMEM)
DMA = pltpu.SemaphoreType.DMA
HEADS = (G, *TILE)
PARTS = (2, 4, 4, *TILE)
SQUARE = (4, HG, 32, COLS)
MIX = (16, HG, 8, 4 * E3)
SEQ = (16, 24, D)


def shape(dims, dtype=bf16):
    return jax.ShapeDtypeStruct(dims, dtype)


def forward_call(q, k, v, inp, cot):
    return pl.pallas_call(
        forward_kernel,
        out_shape=[
            shape(MIX), shape(SEQ), shape(SEQ), shape(PARTS), shape(PARTS), shape(HEADS),
            shape(SQUARE), shape((HG, 32, COLS), f32),
        ],
        in_specs=[ANY] * 5,
        out_specs=[ANY] * 7 + [VM],
        scratch_shapes=[
            pltpu.VMEM(PARTS, bf16), pltpu.VMEM(PARTS, bf16), pltpu.VMEM(HEADS, bf16),
            pltpu.VMEM(SQUARE, bf16), pltpu.VMEM((3, HG, 32, COLS), bf16),
            pltpu.VMEM(SQUARE, bf16), pltpu.VMEM(MIX, bf16),
            DMA((2, 3)), DMA((2, 3)), DMA((2, 4)), DMA((2, 4)), DMA((2, 4)), DMA((2, 4)),
            DMA((6,)), DMA((4,)), DMA((4,)), DMA((3,)), DMA((3,)), DMA((3,)), DMA((3,)),
            DMA((16,)), DMA((16,)), DMA((2, 15)), DMA((2, 15)), DMA((4,)),
        ],
        compiler_params=pltpu.CompilerParams(
            collective_id=0, has_side_effects=True, vmem_limit_bytes=VMEM_LIMIT
        ),
        name="row_forward",
    )(q, k, v, inp, cot)


def backward_call(row_scale, g, k, v, q, w, weights, out, mid):
    return pl.pallas_call(
        functools.partial(backward_kernel, row_scale),
        out_shape=[shape(SEQ), shape(SEQ), shape(HEADS), shape(HEADS), shape(HEADS)],
        in_specs=[ANY] * 8,
        out_specs=[ANY] * 5,
        scratch_shapes=[
            pltpu.VMEM(PARTS, bf16), pltpu.VMEM(PARTS, bf16), pltpu.VMEM(HEADS, bf16),
            pltpu.VMEM(SQUARE, bf16), pltpu.VMEM((HG, 32, COLS), f32), pltpu.VMEM(MIX, bf16),
            pltpu.VMEM(SQUARE, bf16), pltpu.VMEM((3, HG, 32, COLS), bf16),
            pltpu.VMEM(SQUARE, bf16),
            pltpu.VMEM(PARTS, bf16), pltpu.VMEM(PARTS, bf16),
            pltpu.VMEM(PARTS[1:], bf16), pltpu.VMEM(PARTS[1:], bf16),
            pltpu.VMEM((2, 2, 2, *TILE), bf16), pltpu.VMEM((2, 2, 4, *TILE), bf16),
            pltpu.VMEM(HEADS, bf16),
            DMA((2, 3)), DMA((2, 3)), DMA((2, 6)), DMA((2, 6)), DMA((2,)), DMA((2,)),
            DMA((6,)), DMA((4,)), DMA((4,)), DMA((3,)), DMA((3,)), DMA((3,)), DMA((3,)),
            DMA((16,)), DMA((16,)), DMA((2, 15)), DMA((2, 15)), DMA((5,)),
        ],
        compiler_params=pltpu.CompilerParams(
            collective_id=1, has_side_effects=True, vmem_limit_bytes=VMEM_LIMIT
        ),
        name="row_backward",
    )(g, k, v, q, w, weights, out, mid)


def by_seq(values):
    blocks = values.reshape(R3, 16, 8, D)
    return jnp.transpose(blocks, (1, 0, 2, 3)).reshape(SEQ)


def from_seq(blocks):
    return jnp.transpose(blocks.reshape(16, R3, 8, D), (1, 0, 2, 3)).reshape(R3, CB, D)


def on_device(
    inputs, gain_row, w_row_query, w_row_key, w_row_value, w_row_out,
    gain_col, w_col_query, w_col_key, w_col_value, w_col_out, cotangent,
):
    rows = R3 * 16
    row_scale = 1.0 / math.sqrt(DH * rows)
    col_scale = 1.0 / math.sqrt(DH)
    first = normalize(inputs.astype(f32), gain_row).astype(bf16)

    def project_heads(weight, scale=None):
        out = jnp.einsum(
            "rcd,dghe->ghrec", first, weight.reshape(D, G, HG, DH), preferred_element_type=f32
        )
        if scale is not None:
            out = out * scale
        return out.astype(bf16).reshape(HEADS)

    q_send = project_heads(w_row_query, row_scale)
    k_send = project_heads(w_row_key)
    v_send = project_heads(w_row_value)
    mix, inp_c, cot_c, k_all, v_all, q_all, w_all, weights = forward_call(
        q_send, k_send, v_send, by_seq(inputs), by_seq(cotangent)
    )

    mix = mix.reshape(4, 4, HG, 8, 12, DH)
    mixed = jnp.transpose(mix, (0, 4, 3, 1, 2, 5)).reshape(rows, 8, D)
    inp_c = inp_c.reshape(rows, 8, D)
    cot_c = cot_c.reshape(rows, 8, D)

    def project(values, weight):
        return jnp.einsum("rcd,de->rce", values, weight, preferred_element_type=f32)

    def project_back(values, weight):
        return jnp.einsum("rce,de->rcd", values, weight, preferred_element_type=f32)

    def heads_of(values):
        return values.reshape(rows, 8, H, DH)

    middle = (inp_c.astype(f32) + project(mixed, w_row_out)).astype(bf16)
    second = normalize(middle.astype(f32), gain_col).astype(bf16)
    query_h = heads_of((project(second, w_col_query) * col_scale).astype(bf16))
    keys_h = heads_of(project(second, w_col_key).astype(bf16))
    values_h = heads_of(project(second, w_col_value).astype(bf16))
    scores = jnp.einsum("rche,sche->chrs", query_h, keys_h, preferred_element_type=f32)
    col_weights = jax.nn.softmax(scores, axis=-1)
    col_b = col_weights.astype(bf16)
    mixed2 = jnp.einsum("chrs,sche->rche", col_b, values_h, preferred_element_type=f32)
    mixed2 = mixed2.reshape(rows, 8, D).astype(bf16)
    output = (middle.astype(f32) + project(mixed2, w_col_out)).astype(bf16)
    grad_h = heads_of(project_back(cot_c, w_col_out).astype(bf16))
    grad_scores = jnp.einsum("rche,sche->chrs", grad_h, values_h, preferred_element_type=f32)
    grad_values2 = jnp.einsum("chrs,rche->sche", col_b, grad_h, preferred_element_type=f32)
    grad_sb = softmax_back(col_weights, grad_scores).astype(bf16)
    grad_query2 = jnp.einsum("chrs,sche->rche", grad_sb, keys_h, preferred_element_type=f32)
    grad_query2 = grad_query2 * col_scale
    grad_keys2 = jnp.einsum("chrs,rche->sche", grad_sb, query_h, preferred_element_type=f32)

    def joined(values):
        return values.reshape(rows, 8, D).astype(bf16)

    grad_second = (
        project_back(joined(grad_query2), w_col_query)
        + project_back(joined(grad_keys2), w_col_key)
        + project_back(joined(grad_values2), w_col_value)
    )
    grad_middle = (cot_c.astype(f32) + norm_back(middle, gain_col, grad_second)).astype(bf16)
    grad_mixed = project_back(grad_middle, w_row_out).astype(bf16)
    g_send = jnp.transpose(grad_mixed.reshape(4, 12, 8, G, HG, DH), (0, 3, 4, 2, 1, 5)).reshape(MIX)

    out_r, mid_r, grad_q, grad_k, grad_v = backward_call(
        row_scale, g_send, k_all, v_all, q_all, w_all, weights,
        output.reshape(SEQ), grad_middle.reshape(SEQ),
    )
    output = from_seq(out_r)
    grad_middle = from_seq(mid_r)

    def back_heads(grad, weight):
        return jnp.einsum(
            "ghrec,dghe->rcd", grad.reshape(G, HG, R3, DH, CB), weight.reshape(D, G, HG, DH),
            preferred_element_type=f32,
        )

    grad_first = (
        back_heads(grad_q, w_row_query)
        + back_heads(grad_k, w_row_key)
        + back_heads(grad_v, w_row_value)
    )
    grad_inputs = (grad_middle.astype(f32) + norm_back(inputs, gain_row, grad_first)).astype(bf16)
    return (output, grad_inputs)


def solution(mesh):
    token = P("seq", "col", None)
    in_specs = (token,) + (P(),) * 10 + (token,)
    return jax.shard_map(
        on_device, mesh=mesh, in_specs=in_specs, out_specs=(token, token), check_vma=False
    )
```

time: 767 us -> 307 us (0.40)
  waiting for transfers between devices: 487 us -> 0 us
  Pallas kernels: 0 us -> 199 us
  matrix products: 90.7 us -> 36.4 us
  starting transfers between devices: 41.4 us -> 0 us
  local copies, waits for them, and re-layouts: 80 us -> 58.8 us
  blocking collectives: 20.5 us -> 0 us
  other arithmetic: 22.1 us -> 6.31 us
  between operations: 14.8 us -> 1.4 us
    psum x2 -> x0, waiting for transfers between devices: 273 us -> none  [the longest x1 142 us: on_device(): lax.psum(partial_value.astype(jnp.bfloat16), 'seq').astype(jnp.float32)]
    pallas_call x0 -> x2, Pallas kernels: none -> 199 us  [the longest x1 102 us: backward_call(): pl.pallas_call(functools.partial(backward_kernel, row_scale), out_shape=[...]
    all_gather x2 -> x0, waiting for transfers between devices: 102 us -> none  [the longest x1 57.1 us: on_device(): lax.all_gather(keys, 'col', axis=1, tiled=True)]
    reduce_scatter x1 -> x0, waiting for transfers between devices: 63.7 us -> none  [on_device(): lax.psum_scatter(jnp.concatenate([term_keys.reshape(cols_dev * lax.axis_s...]
    dot_general x27 -> x21, matrix products: 85.7 us -> 31.3 us  [the longest x5 7.83 us: project(): return jnp.einsum('rcd,de->rce', values, weight, preferred_element_type=f32)]
    all_to_all x7 -> x0, waiting for transfers between devices: 47.9 us -> none  [the longest x1 12.2 us: on_device(): lax.all_to_all(query2, 'seq', split_axis=1, concat_axis=0, tiled=True)]
    all_to_all x7 -> x0, starting transfers between devices: 41 us -> none  [the longest x1 7.79 us: on_device(): lax.all_to_all(keys2, 'seq', split_axis=1, concat_axis=0, tiled=True)]
    all_to_all x1 -> x0, blocking collectives: 20.5 us -> none  [on_device(): lax.all_to_all(mixed_c, 'seq', split_axis=0, concat_axis=1, tiled=True)]
  transfers between devices with their start and end apart: 12 -> 0, of which waited for: 11 -> 0; matrix products, arithmetic and copies ran while one was open for 14% -> 0% of each run, Pallas kernels for 0% -> 0%
where the time goes in v1:
time: 307 us; the launch traced here: 302 us
  Pallas kernels  199 us (65%)
  local copies, waits for them, and re-layouts  58.8 us (19%)
  matrix products  36.4 us (12%)
  other arithmetic  6.31 us (2%)
    pallas_call x1, Pallas kernels, backward_call(): pl.pallas_call(functools.partial(backward_kernel, row_scale), out_shape=[...  102 us
    pallas_call x1, Pallas kernels, forward_call(): pl.pallas_call(forward_kernel, out_shape=[shape(MIX), shape(SEQ), shape(S...  97.9 us
    convert_element_type x6, local copies, waits for them, and re-layouts, joined(): return values.reshape(rows, 8, D).astype(bf16)  12.6 us
    unnamed x75, local copies, waits for them, and re-layouts  12.2 us
    reshape x4, local copies, waits for them, and re-layouts, heads_of(): return values.reshape(rows, 8, H, DH)  8.95 us
    dot_general x5, matrix products, project(): return jnp.einsum('rcd,de->rce', values, weight, preferred_element_type=f32)  7.83 us

profile of v1, /device:TPU:1, one launch (start us, length us, event | category | flops | bytes accessed | tf_op | source)
XLA Modules:
  0.0 302.4 jit_solution(16782549637771261690)
XLA Ops:
  3.4 1.6 copy.42
  6.9 1.6 copy.44
  10.3 1.6 copy.46
  15.4 97.9 %row_forward.1 = (bf16[16,3,8,768]{3,2,1,0:T(8,128)(2,1)}, bf16[16,24,768]{2,1,0:T(8,128)(2,1)}, bf16[16,24,768]{2,1,0:T(8,128)(2,1)}, bf16[2,4,4,3,192,128]{5,4...) custom-call(bf16[4,3,192,128]{3,2,1,0:T(8,128)(2,1)} %bitcast.157, ...), custom_call_target="tpu_custom_call" | custom-call | tf_op jit(solution)/shard_map/row_forward/pallas_call | solution.py:658
  113.3 1.7 convolution_convert_fusion.5
  115.0 1.9 reshape.170
  117.0 1.9 reshape.166
  118.9 2.2 copy.50
  121.1 3.0 reshape.167
  124.1 2.1 convert_reduce_fusion
  129.8 1.5 convolution_convert_fusion.6
  131.3 2.8 reshape.168
  134.1 1.9 reshape.169
  135.9 2.4 reshape.171
  138.3 5.1 %fusion.71 = (f32[8,12,48]{2,1,0:T(8,128)S(1)}, f32[8,12,48,48]{2,3,1,0:T(8,128)}) fusion(bf16[48,8,12,64]{3,2,1,0:T(8,128)(2,1)} %reshape.168, bf16[48,8,12,64]{3,2,1,0:T(8,128)(2,1)} %reshape.169), kind=kOutput, calls=%fused_computation.104 | convolution fusion | flops 28753968 | bytes 2082816 | tf_op jit(solution)/shard_map/sub | solution.py:760
  143.4 3.1 %fusion.12 = bf16[48,8,12,64]{3,0,2,1:T(8,128)(2,1)S(1)} fusion(bf16[48,8,12,64]{3,2,1,0:T(8,128)(2,1)} %reshape.170, f32[8,12,48,48]{2,3,1,0:T(8,128)} %get-tuple-element.31, f32[8,12,48]{2,1,0:T(8,128)S(1)} %get-tuple-element.30), kind=kOutput, calls=%fused_computation.34 | convolution fusion | flops 29048832 | bytes 2082816 | tf_op jit(solution)/shard_map/chrs,rche->sche/dot_general | solution.py:767
  146.5 1.6 copy.61
  148.1 2.9 convert_element_type.151
  151.0 4.4 %multiply_reduce_fusion = (f32[8,12,48]{2,1,0:T(8,128)S(1)}, f32[8,12,48,48]{2,3,1,0:T(8,128)S(1)}) fusion(f32[8,12,48,48]{2,3,1,0:T(8,128)} %get-tuple-element.31, f32[8,12,48]{2,1,0:T(8,128)S(1)} %get-tuple-element.30, bf16[48,8,12,64]{3,2,1,0:T(8,128)(2,1)} %reshape.171, bf16[48,8,12,64]{3,2,1,0:T(8,128)(2,1)} %reshape.170), kind=kOutput, calls=%fused_computation.3 | convolution fusion | flops 28970496 | bytes 2985984 | tf_op jit(solution)/shard_map/rche,sche->chrs/dot_general | solution.py:766
  155.4 2.2 fusion.10
  161.6 1.6 copy.57
  163.2 2.9 convert_element_type.144
  166.0 1.6 copy.59
  167.6 2.2 convert_element_type.147
  169.8 2.8 copy.65
  172.6 2.3 convert_element_type.156
  174.9 2.8 fusion.20
  184.8 3.2 %reshape.172 = bf16[4,12,8,4,3,64]{5,4,3,2,1,0:T(4,128)(2,1)S(1)} reshape(bf16[48,8,768]{2,1,0:T(8,128)(2,1)} %convolution_convert_fusion.3) | data formatting | bytes 1179648 | tf_op jit(solution)/shard_map/reshape | solution.py:783
  188.0 2.2 copy.62
  190.1 2.9 reshape.173.g_ref
  193.0 101.6 %row_backward.1 = (bf16[16,24,768]{2,1,0:T(8,128)(2,1)}, bf16[16,24,768]{2,1,0:T(8,128)(2,1)}, bf16[4,3,192,128]{3,2,1,0:T(8,128)(2,1)}, bf16[4,3,192,128]{3,2,1,0:T(8,128)(2,1)}, bf16[4,3,192,128]{3,2,1,0:T(8,128)(2,1)}) custom-call(bf16[16,3,8,768]{3,2,1,0:T(8,128)(2,1)} %reshape.173.g_ref, bf16[2,4,4,3,192,128]{5,4,3,2,1,0:T(8,128)(2,1)} %get-tuple-element.18.k_ref, ...), custom_call_target="tpu_custom_call" | custom-call | tf_op jit(solution)/shard_map/row_backward/pallas_call | solution.py:682
  294.6 1.8 convolution_bitcast_fusion
  (106 shorter events, 29.9 us)
Async XLA Ops:
  0.6 126.5 %copy-start = (bf16[768,768]{1,0:T(8,128)(2,1)S(1)}, bf16[768,768]{1,0:T(8,128)(2,1)}, u32[]{:S(2)}) copy-start(bf16[768,768]{1,0:T(8,128)(2,1)} %param.21) | copy-start | bytes 3538948
  3.3 1.7 copy-start.1
  3.4 1.7 copy-start.32
  5.0 1.0 copy-start.4
  8.5 1.0 copy-start.6
  11.9 1.1 copy-start.8
  13.0 1.3 copy-start.23
  15.4 97.9 %copy-start.34 = (bf16[768,768]{1,0:T(8,128)(2,1)S(1)}, bf16[768,768]{1,0:T(8,128)(2,1)}, u32[]{:S(2)}) copy-start(bf16[768,768]{1,0:T(8,128)(2,1)} %param.22) | copy-start | bytes 3538948
  124.1 3.1 %copy-start.31 = (f32[768]{0:T(1024)S(1)}, f32[768]{0:T(1024)}, u32[]{:S(2)}) copy-start(f32[768]{0:T(1024)} %param.18) | copy-start | bytes 9220
  126.3 2.9 copy-start.19
  127.2 2.0 copy-start.27
  127.2 1.3 copy-start.15
  128.5 1.3 copy-start.17
  151.0 4.5 %copy-start.11 = (f32[8,12,48,48]{2,3,1,0:T(8,128)S(1)}, f32[8,12,48,48]{2,3,1,0:T(8,128)}, u32[]{:S(2)}) copy-start(f32[8,12,48,48]{2,3,1,0:T(8,128)} %get-tuple-element.31) | copy-start | bytes 2654212
  151.0 4.5 %copy-start.14 = (bf16[48,8,12,64]{3,2,1,0:T(8,128)(2,1)S(1)}, bf16[48,8,12,64]{3,2,1,0:T(8,128)(2,1)}, u32[]{:S(2)}) copy-start(bf16[48,8,12,64]{3,2,1,0:T(8,128)(2,1)} %reshape.171) | copy-start | bytes 1769476
  157.6 1.4 copy-start.3
  159.0 1.4 copy-start.2
  174.9 2.9 copy-start.13
  174.9 2.9 copy-start.16
  177.8 1.3 copy-start.18
  179.1 1.1 copy-start.12
  179.1 1.1 copy-start.20
  181.0 1.1 copy-start.24
  182.0 1.3 copy-start.35
  193.0 101.6 %copy-start.9 = (bf16[768,768]{0,1:T(8,128)(2,1)S(1)}, bf16[768,768]{0,1:T(8,128)(2,1)}, u32[]{:S(2)}) copy-start(bf16[768,768]{0,1:T(8,128)(2,1)} %copy-done.8) | copy-start | bytes 3538948
  294.6 1.9 copy-start.7
  294.6 1.9 copy-start.26
  296.5 1.3 copy-start.5
  296.5 1.4 copy-start.21
  296.5 1.4 copy-start.33
  297.9 1.1 copy-start.22
  299.8 1.1 copy-start.25
  (4 other events, 3.2 us)

commit v2 on v1

--- a/solution.py
+++ b/solution.py
@@ -638,6 +638,149 @@
     end_mid()
     for copy in gathers:
         copy.wait_send()
+
+
+def lanes(ref):
+    return jnp.concatenate([ref[t] for t in range(6)], axis=1)
+
+
+def put_lanes(ref, values):
+    for t in range(6):
+        ref[t] = values[:, t * 128 : (t + 1) * 128]
+
+
+def column_kernel(
+    col_scale,
+    mix_ref, inp_ref, cot_ref, gain_ref, wro_ref, wq_ref, wk_ref, wv_ref, wco_ref,
+    out_ref, mid_ref, g_ref,
+    WS, X, Xc, Mid, Y, Qs, Ks, Vs, Gs, Ms, sems,
+):
+    loads = []
+    for i, w in enumerate((wro_ref, wco_ref, wq_ref, wk_ref, wv_ref)):
+        copy = pltpu.make_async_copy(w, WS.at[i], sems.at[i])
+        copy.start()
+        loads.append(copy)
+    WRO, WCO, WQ, WK, WV = range(5)
+    low = lax.broadcasted_iota(jnp.int32, (8, 128), 1) < DH
+    swap = lambda v: pltpu.roll(v, DH, 1)
+
+    for x in range(4):
+        for u in range(6):
+            a = mix_ref[x * 4 + (2 * u) // HG, (2 * u) % HG].astype(f32)
+            b = mix_ref[x * 4 + (2 * u + 1) // HG, (2 * u + 1) % HG].astype(f32)
+            for t in range(6):
+                at, bt = a[:, t * 128 : (t + 1) * 128], b[:, t * 128 : (t + 1) * 128]
+                pair = [jnp.where(low, at, swap(bt)), jnp.where(low, swap(at), bt)]
+                rows = (x * 12 + 2 * t) * 8
+                X[rows : rows + 16, u * 128 : (u + 1) * 128] = jnp.concatenate(pair, 0).astype(bf16)
+    loads[WRO].wait()
+    Y[...] = dot(X[...], WS[WRO], 1, 0)
+    gain = gain_ref[...]
+
+    def two(ref, i):
+        return jnp.concatenate([ref[2 * i].astype(f32), ref[2 * i + 1].astype(f32)], axis=0)
+
+    def chunk(i):
+        return pl.ds(pl.multiple_of(i * 48, 48), 48)
+
+    def forward_rows(i, carry):
+        middle = (two(inp_ref, i) + Y[chunk(i), :]).astype(bf16).astype(f32)
+        Mid[chunk(i), :] = middle
+        X[chunk(i), :] = normalize(middle, gain).astype(bf16)
+        Xc[chunk(i), :] = two(cot_ref, i).astype(bf16)
+        return carry
+
+    lax.fori_loop(0, 8, forward_rows, 0)
+    loads[WCO].wait()
+    rounded = lambda v: v.astype(bf16).astype(f32)
+    put_lanes(Gs, rounded(dot(Xc[...], WS[WCO], 1, 1)))
+    loads[WQ].wait()
+    put_lanes(Qs, rounded(dot(X[...], WS[WQ], 1, 0) * col_scale))
+    loads[WK].wait()
+    put_lanes(Ks, rounded(dot(X[...], WS[WK], 1, 0)))
+    loads[WV].wait()
+    put_lanes(Vs, rounded(dot(X[...], WS[WV], 1, 0)))
+
+    head = lax.broadcasted_iota(jnp.int32, (48, 256), 1) // DH
+    masks = [head == i for i in range(4)]
+
+    def stacked(v):
+        return jnp.concatenate([jnp.where(m, v, 0.0) for m in masks], axis=0).astype(bf16)
+
+    def picked(v):
+        total = jnp.where(masks[0], v[:48], 0.0)
+        for i in range(1, 4):
+            total = jnp.where(masks[i], v[i * 48 : (i + 1) * 48], total)
+        return total
+
+    def column(c, carry):
+        rows = pl.ds(c, 48, stride=8)
+        for u in range(3):
+            take = lambda ref: jnp.concatenate([ref[2 * u, rows, :], ref[2 * u + 1, rows, :]], axis=1)
+
+            def give(ref, values):
+                ref[2 * u, rows, :] = values[:, :128]
+                ref[2 * u + 1, rows, :] = values[:, 128:]
+
+            q, k, v, g = take(Qs), take(Ks).astype(bf16), take(Vs).astype(bf16), take(Gs)
+            qs, gs = stacked(q), stacked(g)
+            scores = dot(qs, k, 1, 1)
+            powers = jnp.exp(scores - jnp.max(scores, axis=-1, keepdims=True))
+            weights = powers / jnp.sum(powers, axis=-1, keepdims=True)
+            weights_b = weights.astype(bf16)
+            grad = dot(gs, v, 1, 1)
+            grad = weights * (grad - jnp.sum(weights * grad, axis=-1, keepdims=True))
+            grad_b = grad.astype(bf16)
+            give(Ms, picked(dot(weights_b, v, 1, 0)))
+            give(Vs, dot(weights_b, gs, 0, 0))
+            give(Qs, picked(dot(grad_b, k, 1, 0)) * col_scale)
+            give(Ks, dot(grad_b, qs, 0, 0))
+        return carry
+
+    lax.fori_loop(0, 8, column, 0)
+    Y[...] = dot(lanes(Ms).astype(bf16), WS[WCO], 1, 0)
+
+    def output_rows(i, carry):
+        out = (Mid[chunk(i), :] + Y[chunk(i), :]).astype(bf16)
+        out_ref[2 * i] = out[:24]
+        out_ref[2 * i + 1] = out[24:]
+        return carry
+
+    lax.fori_loop(0, 8, output_rows, 0)
+    Y[...] = dot(lanes(Qs).astype(bf16), WS[WQ], 1, 1)
+    Y[...] += dot(lanes(Ks).astype(bf16), WS[WK], 1, 1)
+    Y[...] += dot(lanes(Vs).astype(bf16), WS[WV], 1, 1)
+
+    def backward_rows(i, carry):
+        grad = two(cot_ref, i) + norm_grad(Mid[chunk(i), :], gain, Y[chunk(i), :])
+        grad = grad.astype(bf16)
+        mid_ref[2 * i] = grad[:24]
+        mid_ref[2 * i + 1] = grad[24:]
+        X[chunk(i), :] = grad
+        return carry
+
+    lax.fori_loop(0, 8, backward_rows, 0)
+    Y[...] = dot(X[...], WS[WRO], 1, 1)
+    for x in range(4):
+        for u in range(6):
+            first, second = [], []
+            for t in range(6):
+                rows = (x * 12 + 2 * t) * 8
+                lo = Y[rows : rows + 8, u * 128 : (u + 1) * 128]
+                hi = Y[rows + 8 : rows + 16, u * 128 : (u + 1) * 128]
+                first.append(jnp.where(low, lo, swap(hi)))
+                second.append(jnp.where(low, swap(lo), hi))
+            g_ref[x * 4 + (2 * u) // HG, (2 * u) % HG] = jnp.concatenate(first, 1).astype(bf16)
+            g_ref[x * 4 + (2 * u + 1) // HG, (2 * u + 1) % HG] = jnp.concatenate(second, 1).astype(bf16)
+
+
+def norm_grad(values, gain, grad):
+    centred = values - jnp.mean(values, axis=-1, keepdims=True)
+    scale = lax.rsqrt(jnp.mean(centred * centred, axis=-1, keepdims=True) + epsilon)
+    unit = centred * scale
+    grad = grad * gain
+    along = jnp.mean(grad * unit, axis=-1, keepdims=True)
+    return scale * (grad - jnp.mean(grad, axis=-1, keepdims=True) - unit * along)
 
 
 ANY = pl.BlockSpec(memory_space=pl.ANY)
@@ -704,6 +847,23 @@
     )(g, k, v, q, w, weights, out, mid)
 
 
+def column_call(col_scale, mix, inp, cot, gain, wro, wq, wk, wv, wco):
+    lane_tiles = pltpu.VMEM((6, 384, 128), f32)
+    return pl.pallas_call(
+        functools.partial(column_kernel, col_scale),
+        out_shape=[shape(SEQ), shape(SEQ), shape(MIX)],
+        in_specs=[VM] * 4 + [ANY] * 5,
+        out_specs=[VM] * 3,
+        scratch_shapes=[
+            pltpu.VMEM((5, D, D), bf16), pltpu.VMEM((384, D), bf16), pltpu.VMEM((384, D), bf16),
+            pltpu.VMEM((384, D), f32), pltpu.VMEM((384, D), f32),
+            lane_tiles, lane_tiles, lane_tiles, lane_tiles, lane_tiles, DMA((5,)),
+        ],
+        compiler_params=pltpu.CompilerParams(vmem_limit_bytes=VMEM_LIMIT),
+        name="column_part",
+    )(mix, inp, cot, gain.reshape(1, D), wro, wq, wk, wv, wco)
+
+
 def by_seq(values):
     blocks = values.reshape(R3, 16, 8, D)
     return jnp.transpose(blocks, (1, 0, 2, 3)).reshape(SEQ)
@@ -737,54 +897,12 @@
         q_send, k_send, v_send, by_seq(inputs), by_seq(cotangent)
     )
 
-    mix = mix.reshape(4, 4, HG, 8, 12, DH)
-    mixed = jnp.transpose(mix, (0, 4, 3, 1, 2, 5)).reshape(rows, 8, D)
-    inp_c = inp_c.reshape(rows, 8, D)
-    cot_c = cot_c.reshape(rows, 8, D)
-
-    def project(values, weight):
-        return jnp.einsum("rcd,de->rce", values, weight, preferred_element_type=f32)
-
-    def project_back(values, weight):
-        return jnp.einsum("rce,de->rcd", values, weight, preferred_element_type=f32)
-
-    def heads_of(values):
-        return values.reshape(rows, 8, H, DH)
-
-    middle = (inp_c.astype(f32) + project(mixed, w_row_out)).astype(bf16)
-    second = normalize(middle.astype(f32), gain_col).astype(bf16)
-    query_h = heads_of((project(second, w_col_query) * col_scale).astype(bf16))
-    keys_h = heads_of(project(second, w_col_key).astype(bf16))
-    values_h = heads_of(project(second, w_col_value).astype(bf16))
-    scores = jnp.einsum("rche,sche->chrs", query_h, keys_h, preferred_element_type=f32)
-    col_weights = jax.nn.softmax(scores, axis=-1)
-    col_b = col_weights.astype(bf16)
-    mixed2 = jnp.einsum("chrs,sche->rche", col_b, values_h, preferred_element_type=f32)
-    mixed2 = mixed2.reshape(rows, 8, D).astype(bf16)
-    output = (middle.astype(f32) + project(mixed2, w_col_out)).astype(bf16)
-    grad_h = heads_of(project_back(cot_c, w_col_out).astype(bf16))
-    grad_scores = jnp.einsum("rche,sche->chrs", grad_h, values_h, preferred_element_type=f32)
-    grad_values2 = jnp.einsum("chrs,rche->sche", col_b, grad_h, preferred_element_type=f32)
-    grad_sb = softmax_back(col_weights, grad_scores).astype(bf16)
-    grad_query2 = jnp.einsum("chrs,sche->rche", grad_sb, keys_h, preferred_element_type=f32)
-    grad_query2 = grad_query2 * col_scale
-    grad_keys2 = jnp.einsum("chrs,rche->sche", grad_sb, query_h, preferred_element_type=f32)
-
-    def joined(values):
-        return values.reshape(rows, 8, D).astype(bf16)
-
-    grad_second = (
-        project_back(joined(grad_query2), w_col_query)
-        + project_back(joined(grad_keys2), w_col_key)
-        + project_back(joined(grad_values2), w_col_value)
+    out_c, mid_c, g_send = column_call(
+        col_scale, mix, inp_c, cot_c, gain_col, w_row_out, w_col_query, w_col_key, w_col_value, w_col_out
     )
-    grad_middle = (cot_c.astype(f32) + norm_back(middle, gain_col, grad_second)).astype(bf16)
-    grad_mixed = project_back(grad_middle, w_row_out).astype(bf16)
-    g_send = jnp.transpose(grad_mixed.reshape(4, 12, 8, G, HG, DH), (0, 3, 4, 2, 1, 5)).reshape(MIX)
-
     out_r, mid_r, grad_q, grad_k, grad_v = backward_call(
         row_scale, g_send, k_all, v_all, q_all, w_all, weights,
-        output.reshape(SEQ), grad_middle.reshape(SEQ),
+        out_c, mid_c,
     )
     output = from_seq(out_r)
     grad_middle = from_seq(mid_r)

time: 307 us -> 250 us (0.81); the launches traced: 302 us -> 250 us
  local copies, waits for them, and re-layouts: 58.8 us -> 10.3 us
  matrix products: 36.4 us -> 6.18 us
  Pallas kernels: 199 us -> 228 us
    pallas_call x0 -> x1, Pallas kernels: none -> 28.3 us  [column_call(): pl.pallas_call(functools.partial(column_kernel, col_scale), out_shape=[sh...]
    dot_general x15 -> x0, matrix products: 25.2 us -> none  [the longest x5 7.83 us: project(): return jnp.einsum('rcd,de->rce', values, weight, preferred_element_type=f32)]
    reshape x8 -> x1, local copies, waits for them, and re-layouts: 19.9 us -> 0.6 us  [column_call(): gain.reshape(1, D)]
    convert_element_type x8 -> x0, local copies, waits for them, and re-layouts: 17.7 us -> none  [the longest x6 12.6 us: joined(): return values.reshape(rows, 8, D).astype(bf16)]
    unnamed x75 -> x25, local copies, waits for them, and re-layouts: 12.2 us -> 5.24 us
    sub x1 -> x0, matrix products: 5.08 us -> none  [on_device(): col_weights = jax.nn.softmax(scores, axis=-1)]
    transpose x2 -> x0, local copies, waits for them, and re-layouts: 4.33 us -> none  [the longest x1 2.17 us: on_device(): jnp.transpose(grad_mixed.reshape(4, 12, 8, G, HG, DH), (0, 3, 4, 2, 1, 5))]
where the time goes in v2:
time: 250 us
  Pallas kernels  228 us (91%)
  local copies, waits for them, and re-layouts  10.3 us (4%)
  matrix products  6.18 us (2%)
  other arithmetic  4.48 us (2%)
    pallas_call x1, Pallas kernels, backward_call(): pl.pallas_call(functools.partial(backward_kernel, row_scale), out_shape=[...  102 us
    pallas_call x1, Pallas kernels, forward_call(): pl.pallas_call(forward_kernel, out_shape=[shape(MIX), shape(SEQ), shape(S...  97.8 us
    pallas_call x1, Pallas kernels, column_call(): pl.pallas_call(functools.partial(column_kernel, col_scale), out_shape=[sh...  28.3 us
    unnamed x25, local copies, waits for them, and re-layouts  5.24 us

profile of v2, /device:TPU:1, one launch (start us, length us, event | category | flops | bytes accessed | tf_op | source)
XLA Modules:
  0.0 249.7 jit_solution(17257761320810448859)
XLA Ops:
  0.6 0.0 copy-start
  0.6 0.0 copy-start.4
  0.7 1.4 convert_reduce_fusion
  2.0 1.4 fusion.11
  3.4 0.0 copy-start.1
  3.4 0.0 copy-start.10
  3.4 0.6 copy.32
  4.1 0.4 copy-done.1
  4.5 0.9 fusion.8
  5.4 0.9 copy.33
  6.3 1.6 copy.34
  7.8 0.9 fusion.9
  8.8 0.1 copy-done.2
  8.8 0.9 copy.35
  9.7 1.6 copy.30
  11.3 0.9 fusion.10
  12.2 0.9 copy.31
  13.1 1.1 copy_bitcast_fusion.1
  14.1 97.8 %row_forward.1 = (bf16[16,3,8,768]{3,2,1,0:T(8,128)(2,1)}, bf16[16,24,768]{2,1,0:T(8,128)(2,1)}, bf16[16,24,768]{2,1,0:T(8,128)(2,1)}, bf16[2,4,4,3,192,128]{5,4...) custom-call(bf16[4,3,192,128]{3,2,1,0:T(8,128)(2,1)} %bitcast.101, ...), custom_call_target="tpu_custom_call" | custom-call | tf_op jit(solution)/shard_map/row_forward/pallas_call | solution.py:801
  111.9 0.6 reshape.96.gain_ref
  112.5 28.3 %column_part.1 = (bf16[16,24,768]{2,1,0:T(8,128)(2,1)}, bf16[16,24,768]{2,1,0:T(8,128)(2,1)}, bf16[16,3,8,768]{3,2,1,0:T(8,128)(2,1)}) custom-call(bf16[16,3,8,768]{3,2,1,0:T(8,128)(2,1)} %get-tuple-element.18.mix_ref, bf16[16,24,768]{2,1,0:T(8,128)(2,1)} %get-tuple-element.19.inp_ref, bf16[16,24,768]{2,1,0:T(8,128)(2,1)} %get-tuple-element.20.cot_ref, ...), custom_call_target="tpu_custom_call" | custom-call | tf_op jit(solution)/shard_map/column_part/pallas_call | solution.py:852
  140.8 101.8 %row_backward.1 = (bf16[16,24,768]{2,1,0:T(8,128)(2,1)}, bf16[16,24,768]{2,1,0:T(8,128)(2,1)}, bf16[4,3,192,128]{3,2,1,0:T(8,128)(2,1)}, bf16[4,3,192,128]{3,2,1,0:T(8,128)(2,1)}, bf16[4,3,192,128]{3,2,1,0:T(8,128)(2,1)}) custom-call(bf16[16,3,8,768]{3,2,1,0:T(8,128)(2,1)} %get-tuple-element.21.g_ref, ...), custom_call_target="tpu_custom_call" | custom-call | tf_op jit(solution)/shard_map/row_backward/pallas_call | solution.py:825
  242.6 1.8 convolution_bitcast_fusion.1
  244.5 0.0 copy-done.3
  244.5 0.0 copy-done.8
  244.5 0.7 convolution_bitcast_fusion
  245.2 0.4 copy-done.5
  245.6 0.9 fusion.14
  246.5 0.5 fusion.17
  247.0 0.6 copy-done.7
  247.6 1.3 fusion.15
  248.8 0.9 copy_bitcast_fusion
  (16 shorter events, 0.1 us)
Async XLA Ops:
  0.6 12.4 %copy-start = (bf16[3,128,768]{2,1,0:T(8,128)(2,1)S(1)}, bf16[3,128,768]{2,1,0:T(8,128)(2,1)}, u32[]{:S(2)}) copy-start(bf16[3,128,768]{2,1,0:T(8,128)(2,1)} %param.23) | copy-start | bytes 1769476
  0.6 2.7 %copy-start.4 = (bf16[768,768]{1,0:T(8,128)(2,1)S(1)}, bf16[768,768]{1,0:T(8,128)(2,1)}, u32[]{:S(2)}) copy-start(bf16[768,768]{1,0:T(8,128)(2,1)} %param.15) | copy-start | bytes 3538948
  3.4 1.1 copy-start.1
  3.4 1.1 copy-start.10
  7.8 1.0 copy-start.2
  14.1 97.8 %copy-start.9 = (f32[768]{0:T(1024)S(1)}, f32[768]{0:T(1024)}, u32[]{:S(2)}) copy-start(f32[768]{0:T(1024)} %param.18) | copy-start | bytes 9220
  242.6 1.9 copy-start.3
  242.6 1.9 copy-start.8
  244.5 1.1 copy-start.5
  246.5 1.1 copy-start.7
  247.6 1.3 copy-start.6

commit v3 on v0

v3 whole, which is shorter than its diff:
```python
import functools
import math

import jax
import jax.numpy as jnp
from jax import lax
from jax.experimental import pallas as pl
from jax.experimental.pallas import tpu as pltpu
from jax.sharding import PartitionSpec as P

D = 768
H = 12
DH = 64
HG = 3
R3 = 3
E3 = R3 * DH
CB = 128
COLS = 1024
TILE = (E3, CB)
TOKENS = 384
MESH = pl.DeviceIdType.MESH

epsilon = 1e-05
f32 = jnp.float32
bf16 = jnp.bfloat16


def normalize(values, gain):
    center = jnp.mean(values, axis=-1, keepdims=True)
    centred = values - center
    spread = jnp.mean(centred * centred, axis=-1, keepdims=True)
    return centred * lax.rsqrt(spread + epsilon) * gain


def norm_grad(values, gain, grad):
    centred = values - jnp.mean(values, axis=-1, keepdims=True)
    scale = lax.rsqrt(jnp.mean(centred * centred, axis=-1, keepdims=True) + epsilon)
    unit = centred * scale
    grad = grad * gain
    along = jnp.mean(grad * unit, axis=-1, keepdims=True)
    return scale * (grad - jnp.mean(grad, axis=-1, keepdims=True) - unit * along)


def dot(a, b, ca, cb):
    return lax.dot_general(a, b, (((ca,), (cb,)), ((), ())), preferred_element_type=f32)


class Place:
    def __init__(self):
        s, q = lax.axis_index("seq"), lax.axis_index("col")
        self.s, self.q = s, q
        self.x, self.yh, self.c = lax.div(s, 4), lax.rem(lax.div(s, 2), 2), lax.rem(s, 2)
        self.yl, self.z = lax.div(q, 4), lax.rem(q, 4)
        self.y = self.yh * 2 + self.yl
        self.block = self.yh * 2 + self.c
        self.zh, self.zl = lax.div(self.z, 2), lax.rem(self.z, 2)
        self.same = (self.block == self.z, self.yl == self.c, self.yl == self.c)

    def at(self, x=None, yh=None, c=None, yl=None, z=None):
        pick = lambda new, old: old if new is None else new
        x, yh, c = pick(x, self.x), pick(yh, self.yh), pick(c, self.c)
        yl, z = pick(yl, self.yl), pick(z, self.z)
        return {"seq": (x * 2 + yh) * 2 + c, "col": yl * 4 + z}

    def along_x(self, k):
        x = lax.rem(self.x + k, 4)
        return x, self.at(x=x)

    def along_z(self, k):
        z = lax.rem(self.z + k, 4)
        return z, self.at(z=z)

    def along_y(self, k):
        y = lax.rem(self.y + k, 4)
        return y, self.at(yh=lax.div(y, 2), yl=lax.rem(y, 2))

    def along_seq(self, k):
        s = lax.rem(self.s + k, 16)
        return s, {"seq": s, "col": self.q}

    def sibling(self):
        return self.at(c=1 - self.c)

    def split(self, h):
        return (self.z, self.along_z) if h == 0 else (self.y, self.along_y)

    def ring(self, h):
        return (self.y, self.along_y) if h == 0 else (self.z, self.along_z)

    def head(self, h, i):
        return i if h == 0 else 4 + 2 * i + (h - 1)

    def owner(self, h, k):
        s = lax.rem(self.s + k, 16)
        col = self.yl * 4 + self.block if h == 0 else self.c * 4 + self.z
        return s, {"seq": s, "col": col}

    def holder(self, h, k):
        x = lax.rem(self.x + k // 4, 4)
        i = self.split(h)[1](k % 4)[0]
        if h == 0:
            device = self.at(x=x, yh=self.zh, c=self.zl, z=i)
        else:
            device = self.at(x=x, yh=lax.div(i, 2), yl=lax.rem(i, 2), c=self.yl)
        return x * 4 + i, i, device

    def rows_of(self, h, b):
        yh, c = lax.div(b, 2), lax.rem(b, 2)
        return self.at(yh=yh, c=c, z=self.block) if h == 0 else self.at(yh=yh, yl=self.c, c=c)


def remote(src, dst, send, recv, device):
    return pltpu.make_async_remote_copy(
        src_ref=src, dst_ref=dst, send_sem=send, recv_sem=recv, device_id=device, device_id_type=MESH
    )


class Route:
    def __init__(self, src, dst, send, recv, device, land, landed, same=None, loc=None):
        self.out = remote(src, dst, send, recv, device)
        self.into = remote(land, land, send, landed, device)
        self.same = same
        if same is not None:
            self.own = pltpu.make_async_copy(src, dst, loc)

    def either(self, here, there):
        if self.same is None:
            there()
        else:
            pl.when(self.same)(here)
            pl.when(jnp.logical_not(self.same))(there)

    def start(self):
        self.either(lambda: self.own.start(), self.out.start)

    def got(self):
        self.either(lambda: self.own.wait(), self.into.wait_recv)

    def end(self):
        self.either(lambda: None, self.out.wait_send)


def each(routes, what):
    for route in routes:
        getattr(route, what)()


def enter(p):
    barrier = pltpu.get_barrier_semaphore()

    def greet(device):
        pl.semaphore_signal(barrier, inc=1, device_id=device, device_id_type=MESH)

    for k in range(1, 4):
        greet(p.along_z(k)[1])
        greet(p.along_y(k)[1])
    for k in range(1, 16):
        greet(p.along_seq(k)[1])
    for h in range(2):
        for k in range(1, 16):
            greet(p.owner(h, k)[1])
            greet(p.holder(h, k)[2])

        @pl.when(jnp.logical_not(p.same[h]))
        def _():
            greet(p.owner(h, 0)[1])
            greet(p.holder(h, 0)[2])

    def wait():
        others = jnp.where(p.same[0], 0, 2) + jnp.where(p.same[1], 0, 2)
        pl.semaphore_wait(barrier, 3 + 3 + 15 + 4 * 15 + others)

    return wait


def exchange_seq(p, src, dst, send, recv, loc):
    routes = []
    for k in range(1, 16):
        s, device = p.along_seq(k)
        other = p.along_seq(16 - k)[0]
        routes.append(
            Route(src.at[s], dst.at[p.s], send.at[k - 1], recv.at[k - 1], device, dst.at[other], recv.at[k - 1])
        )
    own = pltpu.make_async_copy(src.at[p.s], dst.at[p.s], loc)
    own.start()
    each(routes, "start")

    def finish():
        own.wait()
        each(routes, "got")
        each(routes, "end")

    return finish


def x_sum(p, h, L, Rx, send, recv):
    routes = []
    for k in range(1, 4):
        x, device = p.along_x(k)
        slot = Rx.at[h, k - 1]
        routes.append(
            Route(L.at[h, x], slot, send.at[h, k - 1], recv.at[h, k - 1], device, slot, recv.at[h, k - 1])
        )
    each(routes, "start")
    return routes


def x_gather(p, h, W, send, recv):
    routes = []
    for k in range(1, 4):
        device, other = p.along_x(k)[1], p.along_x(4 - k)[0]
        mine = W.at[h, p.x]
        routes.append(
            Route(mine, mine, send.at[h, k - 1], recv.at[h, k - 1], device, W.at[h, other], recv.at[h, k - 1])
        )
    each(routes, "start")
    return routes


class Gather:
    def __init__(self, p, h, src, T, sems, loc):
        self.p, self.src, self.T, self.h = p, src, T, h
        self.ss, self.sr, self.rs, self.rr, self.cs, self.cr = sems
        self.i, self.along = p.split(h)
        self.r, self.around = p.ring(h)
        self.own = pltpu.make_async_copy(src.at[p.head(h, self.i)], T.at[p.c, self.r, self.i], loc)
        self.sent = []

    def send(self, ref, s, r, i, device):
        copy = remote(ref, ref, s.at[i], r.at[i], device)
        copy.start()
        self.sent.append(copy)

    def got(self, ref, s, r, i):
        remote(ref, ref, s.at[i], r.at[i], self.p.sibling()).wait_recv()

    def split_start(self):
        p = self.p
        self.own.start()
        for k in range(1, 4):
            i, device = self.along(k)
            copy = remote(
                self.src.at[p.head(self.h, i)], self.T.at[p.c, self.r, self.i],
                self.ss.at[k - 1], self.sr.at[k - 1], device,
            )
            copy.start()
            self.sent.append(copy)

    def ring_start(self):
        p = self.p
        self.own.wait()
        for k in range(1, 4):
            self.got(self.T.at[p.c, self.r, self.along(4 - k)[0]], self.ss, self.sr, k - 1)
        piece = self.T.at[p.c, self.r]
        self.send(piece, self.rs, self.rr, 0, self.around(1)[1])
        self.send(piece, self.rs, self.rr, 1, self.around(3)[1])
        self.send(piece, self.cs, self.cr, 0, p.sibling())

    def ring_forward(self):
        p = self.p
        left, right = self.T.at[p.c, self.around(3)[0]], self.T.at[p.c, self.around(1)[0]]
        self.got(left, self.rs, self.rr, 0)
        self.send(left.at[pl.ds(0, 2)], self.rs, self.rr, 2, self.around(1)[1])
        self.send(left, self.cs, self.cr, 1, p.sibling())
        self.got(right, self.rs, self.rr, 1)
        self.send(right.at[pl.ds(2, 2)], self.rs, self.rr, 3, self.around(3)[1])
        self.send(right, self.cs, self.cr, 2, p.sibling())

    def ring_finish(self):
        p = self.p
        far = self.T.at[p.c, self.around(2)[0]]
        self.got(far.at[pl.ds(0, 2)], self.rs, self.rr, 2)
        self.got(far.at[pl.ds(2, 2)], self.rs, self.rr, 3)
        self.send(far, self.cs, self.cr, 3, p.sibling())

    def core_wait(self):
        for i, k in enumerate((0, 3, 1, 2)):
            self.got(self.T.at[1 - self.p.c, self.around(k)[0]], self.cs, self.cr, i)

    def end(self):
        for copy in self.sent:
            copy.wait_send()


def add_into(T, index, others, z0, z1):
    def step(z, carry):
        a = T[index + (z + z0,)].astype(f32)
        for ref, at in others:
            a = a + ref[at + (z,)].astype(f32)
        T[index + (z + z0,)] = a.astype(bf16)
        return carry

    lax.fori_loop(0, z1 - z0, step, 0)


class Scatter:
    def __init__(self, p, h, T, C, far, near, out, sems, loc):
        self.p, self.h, self.T, self.C, self.far, self.near, self.out = p, h, T, C, far, near, out
        self.ss, self.sr, self.rs, self.rr, self.cs, self.cr = sems
        self.i, self.along = p.split(h)
        self.r, self.around = p.ring(h)
        mine = p.head(h, self.i)
        self.own = pltpu.make_async_copy(T.at[p.c, self.r, self.i], out.at[mine], loc)
        self.sent = []

    def send(self, src, dst, s, r, device):
        copy = remote(src, dst, s, r, device)
        copy.start()
        self.sent.append(copy)

    def got(self, dst, s, r):
        remote(dst, dst, s, r, self.p.sibling()).wait_recv()

    def core_start(self):
        self.send(self.T.at[1 - self.p.c], self.C, self.cs, self.cr, self.p.sibling())

    def ring_start(self):
        c, T, rs, rr = self.p.c, self.T, self.rs, self.rr
        self.got(self.C, self.cs, self.cr)
        r2, (r1, d1), (r3, d3) = self.around(2)[0], self.around(1), self.around(3)
        lo, hi = pl.ds(0, 2), pl.ds(2, 2)
        add_into(T, (c, r2), [(self.C, (r2,))], 0, 4)
        self.send(T.at[c, r2, lo], self.far.at[0], rs.at[0], rr.at[0], d1)
        self.send(T.at[c, r2, hi], self.far.at[1], rs.at[1], rr.at[1], d3)
        add_into(T, (c, r1), [(self.C, (r1,))], 0, 4)
        add_into(T, (c, r3), [(self.C, (r3,))], 0, 4)
        self.send(T.at[c, r1, hi], self.near.at[0, hi], rs.at[2], rr.at[2], d1)
        self.send(T.at[c, r3, lo], self.near.at[1, lo], rs.at[3], rr.at[3], d3)
        add_into(T, (c, self.r), [(self.C, (self.r,))], 0, 4)

    def ring_forward(self):
        c, T, rs, rr = self.p.c, self.T, self.rs, self.rr
        (r1, d1), (r3, d3) = self.around(1), self.around(3)
        lo, hi = pl.ds(0, 2), pl.ds(2, 2)
        self.got(self.far.at[0], rs.at[0], rr.at[0])
        add_into(T, (c, r1), [(self.far, (0,))], 0, 2)
        self.send(T.at[c, r1, lo], self.near.at[0, lo], rs.at[4], rr.at[4], d1)
        self.got(self.far.at[1], rs.at[1], rr.at[1])
        add_into(T, (c, r3), [(self.far, (1,))], 2, 4)
        self.send(T.at[c, r3, hi], self.near.at[1, hi], rs.at[5], rr.at[5], d3)

    def ring_finish(self):
        p, c, T, rs, rr = self.p, self.p.c, self.T, self.rs, self.rr
        lo, hi = pl.ds(0, 2), pl.ds(2, 2)
        for i, (n, half) in {2: (0, hi), 3: (1, lo), 4: (0, lo), 5: (1, hi)}.items():
            self.got(self.near.at[n, half], rs.at[i], rr.at[i])
        add_into(T, (c, self.r), [(self.near, (0,)), (self.near, (1,))], 0, 4)
        self.own.start()
        slot = self.out.at[p.head(self.h, self.i)]
        for k in range(1, 4):
            i, device = self.along(k)
            self.send(T.at[c, self.r, i], slot, self.ss.at[k - 1], self.sr.at[k - 1], device)

    def end(self):
        self.own.wait()
        for k in range(1, 4):
            i = self.along(4 - k)[0]
            self.got(self.out.at[self.p.head(self.h, i)], self.ss.at[k - 1], self.sr.at[k - 1])
        for copy in self.sent:
            copy.wait_send()


def tile_of(T, h, b, j):
    y, z = (b // 2) * 2 + j // 4, j % 4
    return (h, b % 2, y, z) if h == 0 else (h, b % 2, z, y)


def column_tile(T, h, j):
    return jnp.concatenate([T[tile_of(T, h, b, j)] for b in range(4)], axis=0)


def lanes(ref):
    return jnp.concatenate([ref[t] for t in range(6)], axis=1)


def put_lanes(ref, values):
    for t in range(6):
        ref[t] = values[:, t * 128 : (t + 1) * 128]


WRK, WRQ, WRV, WRO, WCO, WCQ, WCK, WCV = range(8)


def layer_kernel(
    row_scale, col_scale,
    inp_ref, cot_ref, gain_row_ref, gain_col_ref,
    wrk_ref, wrq_ref, wrv_ref, wro_ref, wco_ref, wcq_ref, wck_ref, wcv_ref,
    out_ref, grad_ref,
    WS, K, V, Qf, QS, KS, VS, L, Rx, W, Wg, Pw, M, Mix, Gm,
    TS, InC, CotC, OutR, MidR,
    C, far, near, GQS, GQ, GK, GV,
    X, Xc, Mid, Y, Qs, Ks, Vs, Gs,
    wsem, fs, bs, loc, qs, qr, xs, xr, gs, gr, ms, mr, ts, tr,
    bqs, bqr, bxs, bxr, bgs, bgr, bms, bmr,
):
    heads = range(HG)
    p = Place()
    loads = []
    weight_refs = (wrk_ref, wrq_ref, wrv_ref, wro_ref, wco_ref, wcq_ref, wck_ref, wcv_ref)
    for i, w in enumerate(weight_refs):
        copy = pltpu.make_async_copy(w, WS.at[i], wsem.at[i])
        copy.start()
        loads.append(copy)
    barrier_wait = enter(p)
    gain_row, gain_col = gain_row_ref[...], gain_col_ref[...]

    def strip(i):
        return pl.ds(pl.multiple_of(i * 32, 32), 32)

    def of_rows(ref, i):
        return ref[lax.div(i, 4), strip(lax.rem(i, 4)), :].astype(f32)

    def first_rows(i, carry):
        X[strip(i), :] = normalize(of_rows(inp_ref, i), gain_row).astype(bf16)
        return carry

    lax.fori_loop(0, 12, first_rows, 0)

    def project_tiles(weight, dst, scale=None):
        loads[weight].wait()
        for r in range(R3):
            part = dot(X[r * CB : (r + 1) * CB, :], WS[weight], 1, 0)
            if scale is not None:
                part = part * scale
            part = part.T.astype(bf16)
            for head in range(H):
                dst[head, r * DH : (r + 1) * DH, :] = part[head * DH : (head + 1) * DH]

    def gathers_of(t, src, T):
        return [
            Gather(p, h, src, T.at[h], [fs.at[t, h, pl.ds(a, n)] for a, n in SEMS_F], loc.at[t * 3 + h])
            for h in heads
        ]

    keys, vals = gathers_of(0, KS, K), gathers_of(1, VS, V)
    project_tiles(WRK, KS)
    barrier_wait()
    for h in heads:
        keys[h].split_start()
    project_tiles(WRQ, QS, row_scale)
    queries = []
    for h in heads:
        for k in range(4):
            i = p.split(h)[1](k)[0]
            if h == 0:
                device = p.at(yh=p.zh, c=p.zl, z=i)
            else:
                device = p.at(yh=lax.div(i, 2), yl=lax.rem(i, 2), c=p.yl)
            b = lax.rem(p.block + k, 4)
            queries.append(
                Route(
                    QS.at[p.head(h, i)], Qf.at[h, p.block], qs.at[h, k], qr.at[h, p.block], device,
                    Qf.at[h, b], qr.at[h, b], p.same[h] if k == 0 else None, loc.at[6 + h],
                )
            )
    each(queries, "start")
    keys[0].ring_start()
    keys[1].ring_start()
    project_tiles(WRV, VS)
    for h in heads:
        vals[h].split_start()
    keys[0].ring_forward()
    keys[1].ring_forward()
    keys[2].ring_start()

    def by_seq(ref, dst):
        for s in range(16):
            part = [ref[r, s * 8 : (s + 1) * 8, :].astype(f32) for r in range(R3)]
            dst[s] = jnp.concatenate(part, axis=0).astype(bf16)

    by_seq(inp_ref, TS.at[0])
    by_seq(cot_ref, TS.at[1])
    end_inp = exchange_seq(p, TS.at[0], InC, ts.at[0], tr.at[0], loc.at[9])
    end_cot = exchange_seq(p, TS.at[1], CotC, ts.at[1], tr.at[1], loc.at[10])
    vals[0].ring_start()

    def logits(h):
        qt = jnp.concatenate([Qf[h, b] for b in range(4)], axis=0)
        for j in range(8):
            part = dot(qt, column_tile(K, h, j), 0, 0).astype(bf16)
            L[h, :, :, j * CB : (j + 1) * CB] = part.reshape(4, 32, CB)
        return x_sum(p, h, L, Rx, xs, xr)

    def weigh(h):
        each(sums[h], "got")
        total = L[h, p.x].astype(f32)
        for k in range(3):
            total = total + Rx[h, k].astype(f32)
        powers = jnp.exp(total - jnp.max(total, axis=-1, keepdims=True))
        weights = powers / jnp.sum(powers, axis=-1, keepdims=True)
        Pw[h] = weights
        W[h, p.x] = weights.astype(bf16)
        return x_gather(p, h, W, gs, gr)

    def whole(ref, h):
        return jnp.concatenate([ref[h, x] for x in range(4)], axis=0)

    def mix(h):
        each(shares[h], "got")
        v = jnp.concatenate([column_tile(V, h, j) for j in range(8)], axis=1)
        M[h] = dot(whole(W, h), v, 1, 1).reshape(16, 8, 4 * E3).astype(bf16)
        routes = []
        mine = p.x * 4 + p.split(h)[0]
        for k in range(16):
            s, device = p.owner(h, k)
            slot = p.holder(h, k)[0]
            routes.append(
                Route(
                    M.at[h, s], Mix.at[h, mine], ms.at[h, k], mr.at[h, mine], device,
                    Mix.at[h, slot], mr.at[h, slot], p.same[h] if k == 0 else None, loc.at[11 + h],
                )
            )
        each(routes, "start")
        return routes

    sums, shares, mixes = {}, {}, {}
    keys[0].ring_finish()
    keys[0].core_wait()
    each(queries, "got")
    sums[0] = logits(0)
    keys[1].ring_finish()
    keys[2].ring_forward()
    vals[1].ring_start()
    keys[1].core_wait()
    sums[1] = logits(1)
    vals[0].ring_forward()
    shares[0] = weigh(0)
    keys[2].ring_finish()
    keys[2].core_wait()
    sums[2] = logits(2)
    vals[0].ring_finish()
    shares[1] = weigh(1)
    vals[1].ring_forward()
    vals[2].ring_start()
    shares[2] = weigh(2)
    vals[0].core_wait()
    mixes[0] = mix(0)
    vals[1].ring_finish()
    vals[2].ring_forward()
    vals[1].core_wait()
    mixes[1] = mix(1)
    vals[2].ring_finish()
    vals[2].core_wait()
    mixes[2] = mix(2)
    end_inp()
    end_cot()

    low = lax.broadcasted_iota(jnp.int32, (8, 128), 1) < DH
    swap = lambda v: pltpu.roll(v, DH, 1)

    def piece(x, head):
        if head < 4:
            return 0, x * 4 + head
        return 1 + (head - 4) % 2, x * 4 + (head - 4) // 2

    def two(ref, i):
        return jnp.concatenate([ref[2 * i].astype(f32), ref[2 * i + 1].astype(f32)], axis=0)

    def chunk(i):
        return pl.ds(pl.multiple_of(i * 48, 48), 48)

    def rounded(v):
        return v.astype(bf16).astype(f32)

    def cot_rows(i, carry):
        Xc[chunk(i), :] = two(CotC, i).astype(bf16)
        return carry

    lax.fori_loop(0, 8, cot_rows, 0)
    loads[WCO].wait()
    put_lanes(Gs, rounded(dot(Xc[...], WS[WCO], 1, 1)))
    for h in heads:
        each(mixes[h], "got")
    for x in range(4):
        for u in range(6):
            a, b = Mix[piece(x, 2 * u)].astype(f32), Mix[piece(x, 2 * u + 1)].astype(f32)
            for t in range(6):
                at, bt = a[:, t * 128 : (t + 1) * 128], b[:, t * 128 : (t + 1) * 128]
                pair = [jnp.where(low, at, swap(bt)), jnp.where(low, swap(at), bt)]
                rows = (x * 12 + 2 * t) * 8
                X[rows : rows + 16, u * 128 : (u + 1) * 128] = jnp.concatenate(pair, 0).astype(bf16)
    loads[WRO].wait()
    Y[...] = dot(X[...], WS[WRO], 1, 0)

    def forward_rows(i, carry):
        middle = rounded(two(InC, i) + Y[chunk(i), :])
        Mid[chunk(i), :] = middle
        X[chunk(i), :] = normalize(middle, gain_col).astype(bf16)
        return carry

    lax.fori_loop(0, 8, forward_rows, 0)
    loads[WCQ].wait()
    put_lanes(Qs, rounded(dot(X[...], WS[WCQ], 1, 0) * col_scale))
    loads[WCK].wait()
    put_lanes(Ks, rounded(dot(X[...], WS[WCK], 1, 0)))
    loads[WCV].wait()
    put_lanes(Vs, rounded(dot(X[...], WS[WCV], 1, 0)))

    head_of = lax.broadcasted_iota(jnp.int32, (48, 256), 1) // DH
    masks = [head_of == i for i in range(4)]

    def stacked(v):
        return jnp.concatenate([jnp.where(m, v, 0.0) for m in masks], axis=0).astype(bf16)

    def picked(v):
        total = jnp.where(masks[0], v[:48], 0.0)
        for i in range(1, 4):
            total = jnp.where(masks[i], v[i * 48 : (i + 1) * 48], total)
        return total

    def column(c, carry):
        rows = pl.ds(c, 48, stride=8)
        for u in range(3):
            take = lambda ref: jnp.concatenate([ref[2 * u, rows, :], ref[2 * u + 1, rows, :]], axis=1)

            def give(ref, values):
                ref[2 * u, rows, :] = values[:, :128]
                ref[2 * u + 1, rows, :] = values[:, 128:]

            q, k, v, g = take(Qs), take(Ks).astype(bf16), take(Vs).astype(bf16), take(Gs)
            q_st, g_st = stacked(q), stacked(g)
            scores = dot(q_st, k, 1, 1)
            powers = jnp.exp(scores - jnp.max(scores, axis=-1, keepdims=True))
            weights = powers / jnp.sum(powers, axis=-1, keepdims=True)
            weights_b = weights.astype(bf16)
            grad = dot(g_st, v, 1, 1)
            grad = weights * (grad - jnp.sum(weights * grad, axis=-1, keepdims=True))
            grad_b = grad.astype(bf16)
            give(Gs, picked(dot(weights_b, v, 1, 0)))
            give(Vs, dot(weights_b, g_st, 0, 0))
            give(Qs, picked(dot(grad_b, k, 1, 0)) * col_scale)
            give(Ks, dot(grad_b, q_st, 0, 0))
        return carry

    lax.fori_loop(0, 8, column, 0)
    Y[...] = dot(lanes(Qs).astype(bf16), WS[WCQ], 1, 1)
    Y[...] += dot(lanes(Ks).astype(bf16), WS[WCK], 1, 1)
    Y[...] += dot(lanes(Vs).astype(bf16), WS[WCV], 1, 1)

    def backward_rows(i, carry):
        grad = two(CotC, i) + norm_grad(Mid[chunk(i), :], gain_col, Y[chunk(i), :])
        grad = grad.astype(bf16)
        TS[1, 2 * i] = grad[:24]
        TS[1, 2 * i + 1] = grad[24:]
        X[chunk(i), :] = grad
        return carry

    lax.fori_loop(0, 8, backward_rows, 0)
    Y[...] = dot(X[...], WS[WRO], 1, 1)
    for h in heads:
        each(mixes[h], "end")
        each(sums[h], "end")
        each(shares[h], "end")
        keys[h].end()
        vals[h].end()
    each(queries, "end")
    for x in range(4):
        for u in range(6):
            even, odd = [], []
            for t in range(6):
                rows = (x * 12 + 2 * t) * 8
                lo = Y[rows : rows + 8, u * 128 : (u + 1) * 128]
                hi = Y[rows + 8 : rows + 16, u * 128 : (u + 1) * 128]
                even.append(jnp.where(low, lo, swap(hi)))
                odd.append(jnp.where(low, swap(lo), hi))
            M[piece(x, 2 * u)] = jnp.concatenate(even, 1).astype(bf16)
            M[piece(x, 2 * u + 1)] = jnp.concatenate(odd, 1).astype(bf16)
    grads = {}
    for h in heads:
        grads[h] = []
        for k in range(16):
            slot, _, device = p.holder(h, k)
            s = p.owner(h, k)[0]
            grads[h].append(
                Route(
                    M.at[h, slot], Gm.at[h, p.s], bms.at[h, k], bmr.at[h, p.s], device,
                    Gm.at[h, s], bmr.at[h, s], p.same[h] if k == 0 else None, loc.at[14 + h],
                )
            )
        each(grads[h], "start")
    Y[...] = dot(lanes(Gs).astype(bf16), WS[WCO], 1, 0)

    def output_rows(i, carry):
        out = (Mid[chunk(i), :] + Y[chunk(i), :]).astype(bf16)
        TS[0, 2 * i] = out[:24]
        TS[0, 2 * i + 1] = out[24:]
        return carry

    lax.fori_loop(0, 8, output_rows, 0)

    def grad_of(h):
        return Gm[h].astype(f32).reshape(CB, 4 * E3).astype(bf16)

    def grad_logits(h):
        each(grads[h], "got")
        g = grad_of(h)
        for j in range(8):
            part = dot(g, column_tile(V, h, j), 1, 0).astype(bf16)
            L[h, :, :, j * CB : (j + 1) * CB] = part.reshape(4, 32, CB)
        return x_sum(p, h, L, Rx, bxs, bxr)

    def spread(T, h, j, tile):
        tile = tile.astype(bf16)
        for b in range(4):
            T[tile_of(T, h, b, j)] = tile[b * E3 : (b + 1) * E3]

    def value_grads(h):
        g, w = grad_of(h), whole(W, h)
        for j in range(8):
            spread(V, h, j, dot(g, w[:, j * CB : (j + 1) * CB], 0, 0))
        vals[h].core_start()

    def weigh_back(h):
        each(sums[h], "got")
        total = L[h, p.x].astype(f32)
        for k in range(3):
            total = total + Rx[h, k].astype(f32)
        weights = Pw[h]
        total = weights * (total - jnp.sum(weights * total, axis=-1, keepdims=True))
        Wg[h, p.x] = total.astype(bf16)
        return x_gather(p, h, Wg, bgs, bgr)

    def query_key_grads(h):
        each(shares[h], "got")
        w = whole(Wg, h)
        kt = jnp.concatenate([column_tile(K, h, j) for j in range(8)], axis=1)
        gq = (dot(kt, w, 1, 1) * row_scale).astype(bf16)
        for b in range(4):
            GQS[h, b] = gq[b * E3 : (b + 1) * E3]
        qt = jnp.concatenate([Qf[h, b] for b in range(4)], axis=0)
        for j in range(8):
            spread(K, h, j, dot(qt, w[:, j * CB : (j + 1) * CB], 1, 0))
        keys[h].core_start()
        routes = []
        own, along = p.split(h)
        mine = p.head(h, own)
        for k in range(4):
            b = lax.rem(p.block + k, 4)
            other = p.head(h, along(k)[0])
            routes.append(
                Route(
                    GQS.at[h, b], GQ.at[mine], bqs.at[h, k], bqr.at[mine], p.rows_of(h, b),
                    GQ.at[other], bqr.at[other], p.same[h] if k == 0 else None, loc.at[17 + h],
                )
            )
        each(routes, "start")
        return routes

    def scatters_of(t, T, out):
        return [
            Scatter(
                p, h, T.at[h], C.at[t, h], far.at[t, h], near.at[t, h], out,
                [bs.at[t, h, pl.ds(a, n)] if n > 1 else bs.at[t, h, a] for a, n in SEMS_B],
                loc.at[20 + t * 3 + h],
            )
            for h in heads
        ]

    vals, keys = scatters_of(0, V, GV), scatters_of(1, K, GK)
    for h in heads:
        sums[h] = grad_logits(h)
    for h in heads:
        value_grads(h)
    vals[0].ring_start()
    vals[1].ring_start()
    shares[0] = weigh_back(0)
    shares[1] = weigh_back(1)
    vals[0].ring_forward()
    shares[2] = weigh_back(2)
    end_out = exchange_seq(p, TS.at[0], OutR, ts.at[2], tr.at[2], loc.at[26])
    end_mid = exchange_seq(p, TS.at[1], MidR, ts.at[3], tr.at[3], loc.at[27])
    vals[1].ring_forward()
    vals[2].ring_start()
    back = [query_key_grads(0)]
    keys[0].ring_start()
    vals[0].ring_finish()
    back.append(query_key_grads(1))
    vals[1].ring_finish()
    vals[2].ring_forward()
    keys[1].ring_start()
    keys[0].ring_forward()
    back.append(query_key_grads(2))
    vals[2].ring_finish()
    keys[2].ring_start()
    keys[0].ring_finish()
    keys[1].ring_forward()

    def unproject(src, weight):
        parts = []
        for r in range(R3):
            part = jnp.concatenate([src[head, r * DH : (r + 1) * DH, :] for head in range(H)], axis=0)
            parts.append(dot(part.astype(f32).T.astype(bf16), WS[weight], 1, 1))
        return parts

    for routes in back:
        each(routes, "got")
    for r, part in enumerate(unproject(GQ, WRQ)):
        Y[r * CB : (r + 1) * CB, :] = part
    keys[1].ring_finish()
    keys[2].ring_forward()
    for h in heads:
        vals[h].end()
    for r, part in enumerate(unproject(GV, WRV)):
        Y[r * CB : (r + 1) * CB, :] += part
    end_out()
    end_mid()
    for r in range(R3):
        part = [OutR[s, r * 8 : (r + 1) * 8, :].astype(f32) for s in range(16)]
        out_ref[r] = jnp.concatenate(part, axis=0).astype(bf16)
        part = [MidR[s, r * 8 : (r + 1) * 8, :].astype(f32) for s in range(16)]
        Mid[r * CB : (r + 1) * CB, :] = jnp.concatenate(part, axis=0)
    keys[2].ring_finish()
    for h in heads:
        keys[h].end()
    for r, part in enumerate(unproject(GK, WRK)):
        Y[r * CB : (r + 1) * CB, :] += part

    def last_rows(i, carry):
        grad = Mid[strip(i), :] + norm_grad(of_rows(inp_ref, i), gain_row, Y[strip(i), :])
        grad_ref[lax.div(i, 4), strip(lax.rem(i, 4)), :] = grad.astype(bf16)
        return carry

    lax.fori_loop(0, 12, last_rows, 0)
    for h in heads:
        each(grads[h], "end")
        each(sums[h], "end")
        each(shares[h], "end")
        each(back[h], "end")


SEMS_F = ((0, 3), (3, 3), (6, 4), (10, 4), (14, 4), (18, 4))
SEMS_B = ((0, 3), (3, 3), (6, 6), (12, 6), (18, 1), (19, 1))
ANY = pl.BlockSpec(memory_space=pl.ANY)
VM = pl.BlockSpec(memory_space=pltpu.VMEM)
DMA = pltpu.SemaphoreType.DMA
VMEM_LIMIT = 62 * 2**20


def layer_call(inputs, cotangent, gain_row, gain_col, weights):
    rows = 16 * R3
    row_scale = 1.0 / math.sqrt(DH * rows)
    col_scale = 1.0 / math.sqrt(DH)
    block = (R3, CB, D)
    parts = pltpu.VMEM((HG, 2, 4, 4, *TILE), bf16)
    tiles = pltpu.VMEM((H, *TILE), bf16)
    mine = pltpu.VMEM((HG, 4, *TILE), bf16)
    square = pltpu.VMEM((HG, 4, 32, COLS), bf16)
    pieces = pltpu.VMEM((HG, 16, 8, 4 * E3), bf16)
    seq = pltpu.VMEM((16, 24, D), bf16)
    tokens_b, tokens_f = pltpu.VMEM((TOKENS, D), bf16), pltpu.VMEM((TOKENS, D), f32)
    lane_tiles = pltpu.VMEM((6, TOKENS, 128), f32)
    three, four, sixteen = DMA((HG, 3)), DMA((HG, 4)), DMA((HG, 16))
    return pl.pallas_call(
        functools.partial(layer_kernel, row_scale, col_scale),
        out_shape=[jax.ShapeDtypeStruct(block, bf16)] * 2,
        in_specs=[VM] * 4 + [ANY] * 8,
        out_specs=[VM] * 2,
        scratch_shapes=[
            pltpu.VMEM((8, D, D), bf16), parts, parts, mine, tiles, tiles, tiles,
            square, pltpu.VMEM((HG, 3, 32, COLS), bf16), square, square,
            pltpu.VMEM((HG, 32, COLS), f32), pieces, pieces, pieces,
            pltpu.VMEM((2, 16, 24, D), bf16), seq, seq, seq, seq,
            pltpu.VMEM((2, HG, 4, 4, *TILE), bf16), pltpu.VMEM((2, HG, 2, 2, *TILE), bf16),
            pltpu.VMEM((2, HG, 2, 4, *TILE), bf16), mine, tiles, tiles, tiles,
            tokens_b, tokens_b, tokens_f, tokens_f, lane_tiles, lane_tiles, lane_tiles, lane_tiles,
            DMA((8,)), DMA((2, HG, 22)), DMA((2, HG, 20)), DMA((28,)),
            four, four, three, three, three, three, sixteen, sixteen, DMA((4, 15)), DMA((4, 15)),
            four, DMA((H,)), three, three, three, three, sixteen, sixteen,
        ],
        compiler_params=pltpu.CompilerParams(
            collective_id=0, has_side_effects=True, vmem_limit_bytes=VMEM_LIMIT
        ),
        name="layer",
    )(inputs, cotangent, gain_row.reshape(1, D), gain_col.reshape(1, D), *weights)


def on_device(
    inputs, gain_row, w_row_query, w_row_key, w_row_value, w_row_out,
    gain_col, w_col_query, w_col_key, w_col_value, w_col_out, cotangent,
):
    weights = (
        w_row_key, w_row_query, w_row_value, w_row_out, w_col_out, w_col_query, w_col_key, w_col_value
    )
    return tuple(layer_call(inputs, cotangent, gain_row, gain_col, weights))


def solution(mesh):
    token = P("seq", "col", None)
    in_specs = (token,) + (P(),) * 10 + (token,)
    return jax.shard_map(
        on_device, mesh=mesh, in_specs=in_specs, out_specs=(token, token), check_vma=False
    )
```

time: 767 us -> 190 us (0.25); the launches traced: 757 us -> 190 us
  waiting for transfers between devices: 487 us -> 0 us
  Pallas kernels: 0 us -> 184 us
  matrix products: 90.7 us -> 0 us
  local copies, waits for them, and re-layouts: 80 us -> 5.33 us
  starting transfers between devices: 41.4 us -> 0 us
  other arithmetic: 22.1 us -> 0 us
  blocking collectives: 20.5 us -> 0 us
  between operations: 14.8 us -> 0.65 us
    psum x2 -> x0, waiting for transfers between devices: 273 us -> none  [the longest x1 142 us: on_device(): lax.psum(partial_value.astype(jnp.bfloat16), 'seq').astype(jnp.float32)]
    pallas_call x0 -> x1, Pallas kernels: none -> 184 us  [layer_call(): pl.pallas_call(functools.partial(layer_kernel, row_scale, col_scale), out...]
    all_gather x2 -> x0, waiting for transfers between devices: 102 us -> none  [the longest x1 57.1 us: on_device(): lax.all_gather(keys, 'col', axis=1, tiled=True)]
    dot_general x27 -> x0, matrix products: 85.7 us -> none  [the longest x1 15.6 us: on_device(): jnp.einsum('hij,rihe->jrhe', grad_lb, query_h, preferred_element_type=f32)]
    reduce_scatter x1 -> x0, waiting for transfers between devices: 63.7 us -> none  [on_device(): lax.psum_scatter(jnp.concatenate([term_keys.reshape(cols_dev * lax.axis_s...]
    all_to_all x7 -> x0, waiting for transfers between devices: 47.9 us -> none  [the longest x1 12.2 us: on_device(): lax.all_to_all(query2, 'seq', split_axis=1, concat_axis=0, tiled=True)]
    all_to_all x7 -> x0, starting transfers between devices: 41 us -> none  [the longest x1 7.79 us: on_device(): lax.all_to_all(keys2, 'seq', split_axis=1, concat_axis=0, tiled=True)]
    convert_element_type x16 -> x0, local copies, waits for them, and re-layouts: 23.5 us -> none  [the longest x2 4.57 us: on_device(): grad_keys_c.reshape(col_shape).astype(bf16)]
  transfers between devices with their start and end apart: 12 -> 0, of which waited for: 11 -> 0; matrix products, arithmetic and copies ran while one was open for 14% -> 0% of each run, Pallas kernels for 0% -> 0%
where the time goes in v3:
time: 190 us
  Pallas kernels  184 us (97%)
  local copies, waits for them, and re-layouts  5.33 us (3%)
    pallas_call x1, Pallas kernels, layer_call(): pl.pallas_call(functools.partial(layer_kernel, row_scale, col_scale), out...  184 us

profile of v3, /device:TPU:1, one launch (start us, length us, event | category | flops | bytes accessed | tf_op | source)
XLA Modules:
  0.0 189.6 jit_solution(9221047952382806349)
XLA Ops:
  0.6 1.3 reshape.10.gain_row_ref
  1.9 1.3 reshape.11.gain_col_ref
  3.2 183.6 %layer.1 = (bf16[3,128,768]{2,1,0:T(8,128)(2,1)}, bf16[3,128,768]{2,1,0:T(8,128)(2,1)}) custom-call(bf16[3,128,768]{2,1,0:T(8,128)(2,1)} %inp_ref.1, bf16[3,128,768]{2,1,0:T(8,128)(2,1)} %cot_ref.1, f32[1,768]{1,0:T(1,128)} %reshape.10.gain_row_ref, f32[1,768]{1,0:T(1,128)} %reshape.11.gain_col_ref, bf16[768,768]{1,0:T(8,128)(2,1)} %wrk_ref.1, ...), custom_call_target="tpu_custom_call" | custom-call | tf_op jit(solution)/shard_map/layer/pallas_call | solution.py:853
  186.8 0.0 copy-start
  186.8 2.0 %copy.16 = bf16[3,128,768]{2,1,0:T(8,128)(2,1)} copy(bf16[3,128,768]{2,1,0:T(8,128)(2,1)} %get-tuple-element.4) | data formatting | bytes 1179648
  188.8 0.0 copy-done
  188.8 0.8 copy.17
Async XLA Ops:
  186.8 2.0 %copy-start = (bf16[3,128,768]{2,1,0:T(8,128)(2,1)S(1)}, bf16[3,128,768]{2,1,0:T(8,128)(2,1)}, u32[]{:S(2)}) copy-start(bf16[3,128,768]{2,1,0:T(8,128)(2,1)} %get-tuple-element.5) | copy-start | bytes 1769476

commit v4 on v3

--- a/solution.py
+++ b/solution.py
@@ -117,27 +117,30 @@
 
 class Route:
     def __init__(self, src, dst, send, recv, device, land, landed, same=None, loc=None):
-        self.out = remote(src, dst, send, recv, device)
-        self.into = remote(land, land, send, landed, device)
         self.same = same
+        if same is not True:
+            self.out = remote(src, dst, send, recv, device)
+            self.into = remote(land, land, send, landed, device)
         if same is not None:
             self.own = pltpu.make_async_copy(src, dst, loc)
 
     def either(self, here, there):
         if self.same is None:
             there()
+        elif self.same is True:
+            here()
         else:
             pl.when(self.same)(here)
             pl.when(jnp.logical_not(self.same))(there)
 
     def start(self):
-        self.either(lambda: self.own.start(), self.out.start)
+        self.either(lambda: self.own.start(), lambda: self.out.start())
 
     def got(self):
-        self.either(lambda: self.own.wait(), self.into.wait_recv)
+        self.either(lambda: self.own.wait(), lambda: self.into.wait_recv())
 
     def end(self):
-        self.either(lambda: None, self.out.wait_send)
+        self.either(lambda: None, lambda: self.out.wait_send())
 
 
 def each(routes, what):
@@ -154,34 +157,36 @@
     for k in range(1, 4):
         greet(p.along_z(k)[1])
         greet(p.along_y(k)[1])
-    for k in range(1, 16):
-        greet(p.along_seq(k)[1])
+        greet(p.along_x(k)[1])
+    greet(p.sibling())
     for h in range(2):
-        for k in range(1, 16):
-            greet(p.owner(h, k)[1])
-            greet(p.holder(h, k)[2])
+        for k in range(1, 4):
+            greet(p.rows_of(h, lax.rem(p.block + k, 4)))
 
         @pl.when(jnp.logical_not(p.same[h]))
         def _():
-            greet(p.owner(h, 0)[1])
-            greet(p.holder(h, 0)[2])
+            greet(p.rows_of(h, p.block))
 
     def wait():
-        others = jnp.where(p.same[0], 0, 2) + jnp.where(p.same[1], 0, 2)
-        pl.semaphore_wait(barrier, 3 + 3 + 15 + 4 * 15 + others)
+        others = jnp.where(p.same[0], 0, 1) + jnp.where(p.same[1], 0, 1)
+        pl.semaphore_wait(barrier, 9 + 1 + 2 * 3 + others)
 
     return wait
 
 
 def exchange_seq(p, src, dst, send, recv, loc):
+    both = pl.ds(0, 2)
     routes = []
     for k in range(1, 16):
         s, device = p.along_seq(k)
-        other = p.along_seq(16 - k)[0]
+        land = dst.at[both, p.along_seq(16 - k)[0]]
         routes.append(
-            Route(src.at[s], dst.at[p.s], send.at[k - 1], recv.at[k - 1], device, dst.at[other], recv.at[k - 1])
+            Route(
+                src.at[both, s], dst.at[both, p.s], send.at[k - 1], recv.at[k - 1], device,
+                land, recv.at[k - 1],
+            )
         )
-    own = pltpu.make_async_copy(src.at[p.s], dst.at[p.s], loc)
+    own = pltpu.make_async_copy(src.at[both, p.s], dst.at[both, p.s], loc)
     own.start()
     each(routes, "start")
 
@@ -217,13 +222,37 @@
     return routes
 
 
+def some(p, h):
+    return 0 if h == 0 else pl.ds(1, 2)
+
+
+def some_of(p, h, i):
+    return i if h == 0 else pl.ds(4 + 2 * i, 2)
+
+
+def split_heads(p, h, src, T, send, recv, loc):
+    i, along = p.split(h)
+    r = p.ring(h)[0]
+    mine = T.at[some(p, h), p.c, r, i]
+    routes = []
+    for k in range(4):
+        to, device = along(k)
+        land = T.at[some(p, h), p.c, r, along((4 - k) % 4)[0]]
+        routes.append(
+            Route(
+                src.at[some_of(p, h, to)], mine, send.at[k], recv.at[k], device, land, recv.at[k],
+                True if k == 0 else None, loc,
+            )
+        )
+    each(routes, "start")
+    return routes
+
+
 class Gather:
-    def __init__(self, p, h, src, T, sems, loc):
-        self.p, self.src, self.T, self.h = p, src, T, h
-        self.ss, self.sr, self.rs, self.rr, self.cs, self.cr = sems
-        self.i, self.along = p.split(h)
+    def __init__(self, p, h, T, sems):
+        self.p, self.T = p, T
+        self.rs, self.rr, self.cs, self.cr = sems
         self.r, self.around = p.ring(h)
-        self.own = pltpu.make_async_copy(src.at[p.head(h, self.i)], T.at[p.c, self.r, self.i], loc)
         self.sent = []
 
     def send(self, ref, s, r, i, device):
@@ -234,23 +263,8 @@
     def got(self, ref, s, r, i):
         remote(ref, ref, s.at[i], r.at[i], self.p.sibling()).wait_recv()
 
-    def split_start(self):
-        p = self.p
-        self.own.start()
-        for k in range(1, 4):
-            i, device = self.along(k)
-            copy = remote(
-                self.src.at[p.head(self.h, i)], self.T.at[p.c, self.r, self.i],
-                self.ss.at[k - 1], self.sr.at[k - 1], device,
-            )
-            copy.start()
-            self.sent.append(copy)
-
     def ring_start(self):
         p = self.p
-        self.own.wait()
-        for k in range(1, 4):
-            self.got(self.T.at[p.c, self.r, self.along(4 - k)[0]], self.ss, self.sr, k - 1)
         piece = self.T.at[p.c, self.r]
         self.send(piece, self.rs, self.rr, 0, self.around(1)[1])
         self.send(piece, self.rs, self.rr, 1, self.around(3)[1])
@@ -387,10 +401,10 @@
     wrk_ref, wrq_ref, wrv_ref, wro_ref, wco_ref, wcq_ref, wck_ref, wcv_ref,
     out_ref, grad_ref,
     WS, K, V, Qf, QS, KS, VS, L, Rx, W, Wg, Pw, M, Mix, Gm,
-    TS, InC, CotC, OutR, MidR,
+    TS, SeqC, SeqR,
     C, far, near, GQS, GQ, GK, GV,
     X, Xc, Mid, Y, Qs, Ks, Vs, Gs,
-    wsem, fs, bs, loc, qs, qr, xs, xr, gs, gr, ms, mr, ts, tr,
+    wsem, ss, sr, fs, bs, loc, qs, qr, xs, xr, gs, gr, ms, mr, ts, tr,
     bqs, bqr, bxs, bxr, bgs, bgr, bms, bmr,
 ):
     heads = range(HG)
@@ -402,7 +416,7 @@
         copy.start()
         loads.append(copy)
     barrier_wait = enter(p)
-    gain_row, gain_col = gain_row_ref[...], gain_col_ref[...]
+    gain_row, gain_col = gain_row_ref[...].reshape(1, D), gain_col_ref[...].reshape(1, D)
 
     def strip(i):
         return pl.ds(pl.multiple_of(i * 32, 32), 32)
@@ -426,20 +440,19 @@
             for head in range(H):
                 dst[head, r * DH : (r + 1) * DH, :] = part[head * DH : (head + 1) * DH]
 
-    def gathers_of(t, src, T):
-        return [
-            Gather(p, h, src, T.at[h], [fs.at[t, h, pl.ds(a, n)] for a, n in SEMS_F], loc.at[t * 3 + h])
-            for h in heads
-        ]
-
-    keys, vals = gathers_of(0, KS, K), gathers_of(1, VS, V)
+    def gathers_of(t, T):
+        return [Gather(p, h, T.at[h], [fs.at[t, h, pl.ds(4 * a, 4)] for a in range(4)]) for h in heads]
+
+    def split_all(t, src, T):
+        return [split_heads(p, h, src, T, ss.at[t, h], sr.at[t, h], loc.at[t * 2 + h]) for h in range(2)]
+
+    keys, vals = gathers_of(0, K), gathers_of(1, V)
     project_tiles(WRK, KS)
     barrier_wait()
-    for h in heads:
-        keys[h].split_start()
+    splits = [split_all(0, KS, K)]
     project_tiles(WRQ, QS, row_scale)
     queries = []
-    for h in heads:
+    for h in range(2):
         for k in range(4):
             i = p.split(h)[1](k)[0]
             if h == 0:
@@ -449,16 +462,17 @@
             b = lax.rem(p.block + k, 4)
             queries.append(
                 Route(
-                    QS.at[p.head(h, i)], Qf.at[h, p.block], qs.at[h, k], qr.at[h, p.block], device,
-                    Qf.at[h, b], qr.at[h, b], p.same[h] if k == 0 else None, loc.at[6 + h],
+                    QS.at[some_of(p, h, i)], Qf.at[some(p, h), p.block], qs.at[h, k], qr.at[h, p.block],
+                    device, Qf.at[some(p, h), b], qr.at[h, b], p.same[h] if k == 0 else None, loc.at[6 + h],
                 )
             )
     each(queries, "start")
+    each(splits[0][0], "got")
     keys[0].ring_start()
+    each(splits[0][1], "got")
     keys[1].ring_start()
     project_tiles(WRV, VS)
-    for h in heads:
-        vals[h].split_start()
+    splits.append(split_all(1, VS, V))
     keys[0].ring_forward()
     keys[1].ring_forward()
     keys[2].ring_start()
@@ -470,8 +484,7 @@
 
     by_seq(inp_ref, TS.at[0])
     by_seq(cot_ref, TS.at[1])
-    end_inp = exchange_seq(p, TS.at[0], InC, ts.at[0], tr.at[0], loc.at[9])
-    end_cot = exchange_seq(p, TS.at[1], CotC, ts.at[1], tr.at[1], loc.at[10])
+    each(splits[1][0], "got")
     vals[0].ring_start()
 
     def logits(h):
@@ -520,6 +533,7 @@
     sums[0] = logits(0)
     keys[1].ring_finish()
     keys[2].ring_forward()
+    each(splits[1][1], "got")
     vals[1].ring_start()
     keys[1].core_wait()
     sums[1] = logits(1)
@@ -532,6 +546,7 @@
     shares[1] = weigh(1)
     vals[1].ring_forward()
     vals[2].ring_start()
+    end_seq = exchange_seq(p, TS, SeqC, ts.at[0], tr.at[0], loc.at[9])
     shares[2] = weigh(2)
     vals[0].core_wait()
     mixes[0] = mix(0)
@@ -542,8 +557,7 @@
     vals[2].ring_finish()
     vals[2].core_wait()
     mixes[2] = mix(2)
-    end_inp()
-    end_cot()
+    end_seq()
 
     low = lax.broadcasted_iota(jnp.int32, (8, 128), 1) < DH
     swap = lambda v: pltpu.roll(v, DH, 1)
@@ -553,8 +567,8 @@
             return 0, x * 4 + head
         return 1 + (head - 4) % 2, x * 4 + (head - 4) // 2
 
-    def two(ref, i):
-        return jnp.concatenate([ref[2 * i].astype(f32), ref[2 * i + 1].astype(f32)], axis=0)
+    def two(n, i):
+        return jnp.concatenate([SeqC[n, 2 * i].astype(f32), SeqC[n, 2 * i + 1].astype(f32)], axis=0)
 
     def chunk(i):
         return pl.ds(pl.multiple_of(i * 48, 48), 48)
@@ -563,7 +577,7 @@
         return v.astype(bf16).astype(f32)
 
     def cot_rows(i, carry):
-        Xc[chunk(i), :] = two(CotC, i).astype(bf16)
+        Xc[chunk(i), :] = two(1, i).astype(bf16)
         return carry
 
     lax.fori_loop(0, 8, cot_rows, 0)
@@ -583,7 +597,7 @@
     Y[...] = dot(X[...], WS[WRO], 1, 0)
 
     def forward_rows(i, carry):
-        middle = rounded(two(InC, i) + Y[chunk(i), :])
+        middle = rounded(two(0, i) + Y[chunk(i), :])
         Mid[chunk(i), :] = middle
         X[chunk(i), :] = normalize(middle, gain_col).astype(bf16)
         return carry
@@ -608,7 +622,7 @@
             total = jnp.where(masks[i], v[i * 48 : (i + 1) * 48], total)
         return total
 
-    def column(c, carry):
+    def column(c):
         rows = pl.ds(c, 48, stride=8)
         for u in range(3):
             take = lambda ref: jnp.concatenate([ref[2 * u, rows, :], ref[2 * u + 1, rows, :]], axis=1)
@@ -619,26 +633,30 @@
 
             q, k, v, g = take(Qs), take(Ks).astype(bf16), take(Vs).astype(bf16), take(Gs)
             q_st, g_st = stacked(q), stacked(g)
-            scores = dot(q_st, k, 1, 1)
-            powers = jnp.exp(scores - jnp.max(scores, axis=-1, keepdims=True))
-            weights = powers / jnp.sum(powers, axis=-1, keepdims=True)
+            scores = dot(k, q_st, 1, 1)
+            powers = jnp.exp(scores - jnp.max(scores, axis=0, keepdims=True))
+            weights = powers / jnp.sum(powers, axis=0, keepdims=True)
             weights_b = weights.astype(bf16)
-            grad = dot(g_st, v, 1, 1)
-            grad = weights * (grad - jnp.sum(weights * grad, axis=-1, keepdims=True))
+            grad = dot(v, g_st, 1, 1)
+            grad = weights * (grad - jnp.sum(weights * grad, axis=0, keepdims=True))
             grad_b = grad.astype(bf16)
-            give(Gs, picked(dot(weights_b, v, 1, 0)))
-            give(Vs, dot(weights_b, g_st, 0, 0))
-            give(Qs, picked(dot(grad_b, k, 1, 0)) * col_scale)
-            give(Ks, dot(grad_b, q_st, 0, 0))
+            give(Gs, picked(dot(weights_b, v, 0, 0)))
+            give(Vs, dot(weights_b, g_st, 1, 0))
+            give(Qs, picked(dot(grad_b, k, 0, 0)) * col_scale)
+            give(Ks, dot(grad_b, q_st, 1, 0))
+
+    def columns(i, carry):
+        column(2 * i)
+        column(2 * i + 1)
         return carry
 
-    lax.fori_loop(0, 8, column, 0)
+    lax.fori_loop(0, 4, columns, 0)
     Y[...] = dot(lanes(Qs).astype(bf16), WS[WCQ], 1, 1)
     Y[...] += dot(lanes(Ks).astype(bf16), WS[WCK], 1, 1)
     Y[...] += dot(lanes(Vs).astype(bf16), WS[WCV], 1, 1)
 
     def backward_rows(i, carry):
-        grad = two(CotC, i) + norm_grad(Mid[chunk(i), :], gain_col, Y[chunk(i), :])
+        grad = two(1, i) + norm_grad(Mid[chunk(i), :], gain_col, Y[chunk(i), :])
         grad = grad.astype(bf16)
         TS[1, 2 * i] = grad[:24]
         TS[1, 2 * i + 1] = grad[24:]
@@ -654,6 +672,8 @@
         keys[h].end()
         vals[h].end()
     each(queries, "end")
+    for routes in splits[0] + splits[1]:
+        each(routes, "end")
     for x in range(4):
         for u in range(6):
             even, odd = [], []
@@ -666,15 +686,15 @@
             M[piece(x, 2 * u)] = jnp.concatenate(even, 1).astype(bf16)
             M[piece(x, 2 * u + 1)] = jnp.concatenate(odd, 1).astype(bf16)
     grads = {}
-    for h in heads:
+    for h in range(2):
         grads[h] = []
         for k in range(16):
             slot, _, device = p.holder(h, k)
             s = p.owner(h, k)[0]
             grads[h].append(
                 Route(
-                    M.at[h, slot], Gm.at[h, p.s], bms.at[h, k], bmr.at[h, p.s], device,
-                    Gm.at[h, s], bmr.at[h, s], p.same[h] if k == 0 else None, loc.at[14 + h],
+                    M.at[some(p, h), slot], Gm.at[some(p, h), p.s], bms.at[h, k], bmr.at[h, p.s], device,
+                    Gm.at[some(p, h), s], bmr.at[h, s], p.same[h] if k == 0 else None, loc.at[14 + h],
                 )
             )
         each(grads[h], "start")
@@ -692,7 +712,8 @@
         return Gm[h].astype(f32).reshape(CB, 4 * E3).astype(bf16)
 
     def grad_logits(h):
-        each(grads[h], "got")
+        if h < 2:
+            each(grads[h], "got")
         g = grad_of(h)
         for j in range(8):
             part = dot(g, column_tile(V, h, j), 1, 0).astype(bf16)
@@ -767,8 +788,6 @@
     shares[1] = weigh_back(1)
     vals[0].ring_forward()
     shares[2] = weigh_back(2)
-    end_out = exchange_seq(p, TS.at[0], OutR, ts.at[2], tr.at[2], loc.at[26])
-    end_mid = exchange_seq(p, TS.at[1], MidR, ts.at[3], tr.at[3], loc.at[27])
     vals[1].ring_forward()
     vals[2].ring_start()
     back = [query_key_grads(0)]
@@ -780,6 +799,7 @@
     keys[1].ring_start()
     keys[0].ring_forward()
     back.append(query_key_grads(2))
+    end_seq = exchange_seq(p, TS, SeqR, ts.at[1], tr.at[1], loc.at[26])
     vals[2].ring_finish()
     keys[2].ring_start()
     keys[0].ring_finish()
@@ -802,12 +822,11 @@
         vals[h].end()
     for r, part in enumerate(unproject(GV, WRV)):
         Y[r * CB : (r + 1) * CB, :] += part
-    end_out()
-    end_mid()
+    end_seq()
     for r in range(R3):
-        part = [OutR[s, r * 8 : (r + 1) * 8, :].astype(f32) for s in range(16)]
+        part = [SeqR[0, s, r * 8 : (r + 1) * 8, :].astype(f32) for s in range(16)]
         out_ref[r] = jnp.concatenate(part, axis=0).astype(bf16)
-        part = [MidR[s, r * 8 : (r + 1) * 8, :].astype(f32) for s in range(16)]
+        part = [SeqR[1, s, r * 8 : (r + 1) * 8, :].astype(f32) for s in range(16)]
         Mid[r * CB : (r + 1) * CB, :] = jnp.concatenate(part, axis=0)
     keys[2].ring_finish()
     for h in heads:
@@ -822,13 +841,13 @@
 
     lax.fori_loop(0, 12, last_rows, 0)
     for h in heads:
-        each(grads[h], "end")
         each(sums[h], "end")
         each(shares[h], "end")
         each(back[h], "end")
-
-
-SEMS_F = ((0, 3), (3, 3), (6, 4), (10, 4), (14, 4), (18, 4))
+    for h in range(2):
+        each(grads[h], "end")
+
+
 SEMS_B = ((0, 3), (3, 3), (6, 6), (12, 6), (18, 1), (19, 1))
 ANY = pl.BlockSpec(memory_space=pl.ANY)
 VM = pl.BlockSpec(memory_space=pltpu.VMEM)
@@ -846,7 +865,7 @@
     mine = pltpu.VMEM((HG, 4, *TILE), bf16)
     square = pltpu.VMEM((HG, 4, 32, COLS), bf16)
     pieces = pltpu.VMEM((HG, 16, 8, 4 * E3), bf16)
-    seq = pltpu.VMEM((16, 24, D), bf16)
+    seq = pltpu.VMEM((2, 16, 24, D), bf16)
     tokens_b, tokens_f = pltpu.VMEM((TOKENS, D), bf16), pltpu.VMEM((TOKENS, D), f32)
     lane_tiles = pltpu.VMEM((6, TOKENS, 128), f32)
     three, four, sixteen = DMA((HG, 3)), DMA((HG, 4)), DMA((HG, 16))
@@ -859,19 +878,19 @@
             pltpu.VMEM((8, D, D), bf16), parts, parts, mine, tiles, tiles, tiles,
             square, pltpu.VMEM((HG, 3, 32, COLS), bf16), square, square,
             pltpu.VMEM((HG, 32, COLS), f32), pieces, pieces, pieces,
-            pltpu.VMEM((2, 16, 24, D), bf16), seq, seq, seq, seq,
+            seq, seq, seq,
             pltpu.VMEM((2, HG, 4, 4, *TILE), bf16), pltpu.VMEM((2, HG, 2, 2, *TILE), bf16),
             pltpu.VMEM((2, HG, 2, 4, *TILE), bf16), mine, tiles, tiles, tiles,
             tokens_b, tokens_b, tokens_f, tokens_f, lane_tiles, lane_tiles, lane_tiles, lane_tiles,
-            DMA((8,)), DMA((2, HG, 22)), DMA((2, HG, 20)), DMA((28,)),
-            four, four, three, three, three, three, sixteen, sixteen, DMA((4, 15)), DMA((4, 15)),
+            DMA((8,)), DMA((2, 2, 4)), DMA((2, 2, 4)), DMA((2, HG, 16)), DMA((2, HG, 20)), DMA((28,)),
+            four, four, three, three, three, three, sixteen, sixteen, DMA((2, 15)), DMA((2, 15)),
             four, DMA((H,)), three, three, three, three, sixteen, sixteen,
         ],
         compiler_params=pltpu.CompilerParams(
             collective_id=0, has_side_effects=True, vmem_limit_bytes=VMEM_LIMIT
         ),
         name="layer",
-    )(inputs, cotangent, gain_row.reshape(1, D), gain_col.reshape(1, D), *weights)
+    )(inputs, cotangent, gain_row, gain_col, *weights)
 
 
 def on_device(

time: 190 us -> 182 us (0.958)
  Pallas kernels: 184 us -> 178 us
  local copies, waits for them, and re-layouts: 5.33 us -> 2.8 us
    pallas_call x1, Pallas kernels: 184 us -> 178 us  [layer_call(): pl.pallas_call(functools.partial(layer_kernel, row_scale, col_scale), out...]
    reshape x2 -> x0, local copies, waits for them, and re-layouts: 2.53 us -> none  [the longest x1 1.27 us: layer_call(): gain_row.reshape(1, D)]
where the time goes in v4:
time: 182 us
  Pallas kernels  178 us (98%)
  local copies, waits for them, and re-layouts  2.8 us (2%)
    pallas_call x1, Pallas kernels, layer_call(): pl.pallas_call(functools.partial(layer_kernel, row_scale, col_scale), out...  178 us

profile of v4, /device:TPU:1, one launch (start us, length us, event | category | flops | bytes accessed | tf_op | source)
XLA Modules:
  0.0 181.6 jit_solution(16821851012174074480)
XLA Ops:
  0.6 178.2 %layer.1 = (bf16[3,128,768]{2,1,0:T(8,128)(2,1)}, bf16[3,128,768]{2,1,0:T(8,128)(2,1)}) custom-call(bf16[3,128,768]{2,1,0:T(8,128)(2,1)} %inp_ref.1, bf16[3,128,768]{2,1,0:T(8,128)(2,1)} %cot_ref.1, f32[768]{0:T(1024)} %gain_row_ref.1, f32[768]{0:T(1024)} %gain_col_ref.1, bf16[768,768]{1,0:T(8,128)(2,1)} %wrk_ref.1, bf16[768,768]{1,0:T(8,128)(2,1)} %wrq_ref.1, ...), custom_call_target="tpu_custom_call" | custom-call | tf_op jit(solution)/shard_map/layer/pallas_call | solution.py:872
  178.8 0.0 copy-start
  178.8 2.0 %copy.16 = bf16[3,128,768]{2,1,0:T(8,128)(2,1)} copy(bf16[3,128,768]{2,1,0:T(8,128)(2,1)} %get-tuple-element.4) | data formatting | bytes 1179648
  180.8 0.0 copy-done
  180.8 0.8 copy.17
Async XLA Ops:
  178.8 2.0 %copy-start = (bf16[3,128,768]{2,1,0:T(8,128)(2,1)S(1)}, bf16[3,128,768]{2,1,0:T(8,128)(2,1)}, u32[]{:S(2)}) copy-start(bf16[3,128,768]{2,1,0:T(8,128)(2,1)} %get-tuple-element.5) | copy-start | bytes 1769476

commit v5 on v4

--- a/solution.py
+++ b/solution.py
@@ -157,8 +157,8 @@
     for k in range(1, 4):
         greet(p.along_z(k)[1])
         greet(p.along_y(k)[1])
-        greet(p.along_x(k)[1])
-    greet(p.sibling())
+    for k in range(1, 16):
+        greet(p.along_seq(k)[1])
     for h in range(2):
         for k in range(1, 4):
             greet(p.rows_of(h, lax.rem(p.block + k, 4)))
@@ -169,7 +169,7 @@
 
     def wait():
         others = jnp.where(p.same[0], 0, 1) + jnp.where(p.same[1], 0, 1)
-        pl.semaphore_wait(barrier, 9 + 1 + 2 * 3 + others)
+        pl.semaphore_wait(barrier, 2 * 3 + 15 + 2 * 3 + others)
 
     return wait
 
@@ -365,11 +365,13 @@
             i, device = self.along(k)
             self.send(T.at[c, self.r, i], slot, self.ss.at[k - 1], self.sr.at[k - 1], device)
 
-    def end(self):
+    def landed(self):
         self.own.wait()
         for k in range(1, 4):
             i = self.along(4 - k)[0]
             self.got(self.out.at[self.p.head(self.h, i)], self.ss.at[k - 1], self.sr.at[k - 1])
+
+    def end(self):
         for copy in self.sent:
             copy.wait_send()
 
@@ -412,9 +414,11 @@
     loads = []
     weight_refs = (wrk_ref, wrq_ref, wrv_ref, wro_ref, wco_ref, wcq_ref, wck_ref, wcv_ref)
     for i, w in enumerate(weight_refs):
-        copy = pltpu.make_async_copy(w, WS.at[i], wsem.at[i])
-        copy.start()
-        loads.append(copy)
+        quarters = [pl.ds(n * (D // 4), D // 4) for n in range(4)]
+        loads.append(
+            [pltpu.make_async_copy(w.at[n], WS.at[i, n], wsem.at[i, k]) for k, n in enumerate(quarters)]
+        )
+    each(loads[WRK], "start")
     barrier_wait = enter(p)
     gain_row, gain_col = gain_row_ref[...].reshape(1, D), gain_col_ref[...].reshape(1, D)
 
@@ -429,9 +433,11 @@
         return carry
 
     lax.fori_loop(0, 12, first_rows, 0)
+    each(loads[WRQ], "start")
+    each(loads[WRV], "start")
 
     def project_tiles(weight, dst, scale=None):
-        loads[weight].wait()
+        each(loads[weight], "wait")
         for r in range(R3):
             part = dot(X[r * CB : (r + 1) * CB, :], WS[weight], 1, 0)
             if scale is not None:
@@ -450,6 +456,15 @@
     project_tiles(WRK, KS)
     barrier_wait()
     splits = [split_all(0, KS, K)]
+
+    def by_seq(ref, dst):
+        for s in range(16):
+            part = [ref[r, s * 8 : (s + 1) * 8, :].astype(f32) for r in range(R3)]
+            dst[s] = jnp.concatenate(part, axis=0).astype(bf16)
+
+    by_seq(inp_ref, TS.at[0])
+    by_seq(cot_ref, TS.at[1])
+    end_seq = exchange_seq(p, TS, SeqC, ts.at[0], tr.at[0], loc.at[9])
     project_tiles(WRQ, QS, row_scale)
     queries = []
     for h in range(2):
@@ -473,17 +488,12 @@
     keys[1].ring_start()
     project_tiles(WRV, VS)
     splits.append(split_all(1, VS, V))
+    for weight in (WCO, WRO, WCQ, WCK, WCV):
+        each(loads[weight], "start")
     keys[0].ring_forward()
     keys[1].ring_forward()
     keys[2].ring_start()
 
-    def by_seq(ref, dst):
-        for s in range(16):
-            part = [ref[r, s * 8 : (s + 1) * 8, :].astype(f32) for r in range(R3)]
-            dst[s] = jnp.concatenate(part, axis=0).astype(bf16)
-
-    by_seq(inp_ref, TS.at[0])
-    by_seq(cot_ref, TS.at[1])
     each(splits[1][0], "got")
     vals[0].ring_start()
 
@@ -546,7 +556,6 @@
     shares[1] = weigh(1)
     vals[1].ring_forward()
     vals[2].ring_start()
-    end_seq = exchange_seq(p, TS, SeqC, ts.at[0], tr.at[0], loc.at[9])
     shares[2] = weigh(2)
     vals[0].core_wait()
     mixes[0] = mix(0)
@@ -554,10 +563,21 @@
     vals[2].ring_forward()
     vals[1].core_wait()
     mixes[1] = mix(1)
+    for h in heads:
+        keys[h].end()
+        each(sums[h], "end")
+    each(queries, "end")
+    for routes in splits[0] + splits[1]:
+        each(routes, "end")
+    each(mixes[0], "end")
     vals[2].ring_finish()
     vals[2].core_wait()
     mixes[2] = mix(2)
     end_seq()
+    for h in heads:
+        vals[h].end()
+        each(shares[h], "end")
+    each(mixes[1], "end")
 
     low = lax.broadcasted_iota(jnp.int32, (8, 128), 1) < DH
     swap = lambda v: pltpu.roll(v, DH, 1)
@@ -581,7 +601,7 @@
         return carry
 
     lax.fori_loop(0, 8, cot_rows, 0)
-    loads[WCO].wait()
+    each(loads[WCO], "wait")
     put_lanes(Gs, rounded(dot(Xc[...], WS[WCO], 1, 1)))
     for h in heads:
         each(mixes[h], "got")
@@ -593,7 +613,7 @@
                 pair = [jnp.where(low, at, swap(bt)), jnp.where(low, swap(at), bt)]
                 rows = (x * 12 + 2 * t) * 8
                 X[rows : rows + 16, u * 128 : (u + 1) * 128] = jnp.concatenate(pair, 0).astype(bf16)
-    loads[WRO].wait()
+    each(loads[WRO], "wait")
     Y[...] = dot(X[...], WS[WRO], 1, 0)
 
     def forward_rows(i, carry):
@@ -603,11 +623,11 @@
         return carry
 
     lax.fori_loop(0, 8, forward_rows, 0)
-    loads[WCQ].wait()
+    each(loads[WCQ], "wait")
     put_lanes(Qs, rounded(dot(X[...], WS[WCQ], 1, 0) * col_scale))
-    loads[WCK].wait()
+    each(loads[WCK], "wait")
     put_lanes(Ks, rounded(dot(X[...], WS[WCK], 1, 0)))
-    loads[WCV].wait()
+    each(loads[WCV], "wait")
     put_lanes(Vs, rounded(dot(X[...], WS[WCV], 1, 0)))
 
     head_of = lax.broadcasted_iota(jnp.int32, (48, 256), 1) // DH
@@ -665,15 +685,7 @@
 
     lax.fori_loop(0, 8, backward_rows, 0)
     Y[...] = dot(X[...], WS[WRO], 1, 1)
-    for h in heads:
-        each(mixes[h], "end")
-        each(sums[h], "end")
-        each(shares[h], "end")
-        keys[h].end()
-        vals[h].end()
-    each(queries, "end")
-    for routes in splits[0] + splits[1]:
-        each(routes, "end")
+    each(mixes[2], "end")
     for x in range(4):
         for u in range(6):
             even, odd = [], []
@@ -799,10 +811,10 @@
     keys[1].ring_start()
     keys[0].ring_forward()
     back.append(query_key_grads(2))
-    end_seq = exchange_seq(p, TS, SeqR, ts.at[1], tr.at[1], loc.at[26])
     vals[2].ring_finish()
     keys[2].ring_start()
     keys[0].ring_finish()
+    end_seq = exchange_seq(p, TS, SeqR, ts.at[1], tr.at[1], loc.at[26])
     keys[1].ring_forward()
 
     def unproject(src, weight):
@@ -819,7 +831,7 @@
     keys[1].ring_finish()
     keys[2].ring_forward()
     for h in heads:
-        vals[h].end()
+        vals[h].landed()
     for r, part in enumerate(unproject(GV, WRV)):
         Y[r * CB : (r + 1) * CB, :] += part
     end_seq()
@@ -828,24 +840,27 @@
         out_ref[r] = jnp.concatenate(part, axis=0).astype(bf16)
         part = [SeqR[1, s, r * 8 : (r + 1) * 8, :].astype(f32) for s in range(16)]
         Mid[r * CB : (r + 1) * CB, :] = jnp.concatenate(part, axis=0)
-    keys[2].ring_finish()
     for h in heads:
-        keys[h].end()
-    for r, part in enumerate(unproject(GK, WRK)):
-        Y[r * CB : (r + 1) * CB, :] += part
-
-    def last_rows(i, carry):
-        grad = Mid[strip(i), :] + norm_grad(of_rows(inp_ref, i), gain_row, Y[strip(i), :])
-        grad_ref[lax.div(i, 4), strip(lax.rem(i, 4)), :] = grad.astype(bf16)
-        return carry
-
-    lax.fori_loop(0, 12, last_rows, 0)
-    for h in heads:
+        vals[h].end()
         each(sums[h], "end")
         each(shares[h], "end")
         each(back[h], "end")
     for h in range(2):
         each(grads[h], "end")
+        keys[h].landed()
+        keys[h].end()
+    keys[2].ring_finish()
+    keys[2].landed()
+    for r, part in enumerate(unproject(GK, WRK)):
+        Y[r * CB : (r + 1) * CB, :] += part
+
+    def last_rows(i, carry):
+        grad = Mid[strip(i), :] + norm_grad(of_rows(inp_ref, i), gain_row, Y[strip(i), :])
+        grad_ref[lax.div(i, 4), strip(lax.rem(i, 4)), :] = grad.astype(bf16)
+        return carry
+
+    lax.fori_loop(0, 12, last_rows, 0)
+    keys[2].end()
 
 
 SEMS_B = ((0, 3), (3, 3), (6, 6), (12, 6), (18, 1), (19, 1))
@@ -882,7 +897,7 @@
             pltpu.VMEM((2, HG, 4, 4, *TILE), bf16), pltpu.VMEM((2, HG, 2, 2, *TILE), bf16),
             pltpu.VMEM((2, HG, 2, 4, *TILE), bf16), mine, tiles, tiles, tiles,
             tokens_b, tokens_b, tokens_f, tokens_f, lane_tiles, lane_tiles, lane_tiles, lane_tiles,
-            DMA((8,)), DMA((2, 2, 4)), DMA((2, 2, 4)), DMA((2, HG, 16)), DMA((2, HG, 20)), DMA((28,)),
+            DMA((8, 4)), DMA((2, 2, 4)), DMA((2, 2, 4)), DMA((2, HG, 16)), DMA((2, HG, 20)), DMA((28,)),
             four, four, three, three, three, three, sixteen, sixteen, DMA((2, 15)), DMA((2, 15)),
             four, DMA((H,)), three, three, three, three, sixteen, sixteen,
         ],

time: 182 us -> 181 us (level)
  no operation moved by 1% of the time
where the time goes in v5:
time: 181 us; the launch traced here: 180 us
  Pallas kernels  177 us (98%)
  local copies, waits for them, and re-layouts  2.8 us (2%)
    pallas_call x1, Pallas kernels, layer_call(): pl.pallas_call(functools.partial(layer_kernel, row_scale, col_scale), out...  177 us

profile of v5, /device:TPU:1, one launch (start us, length us, event | category | flops | bytes accessed | tf_op | source)
XLA Modules:
  0.0 180.5 jit_solution(13225373782612210601)
XLA Ops:
  0.6 177.0 %layer.1 = (bf16[3,128,768]{2,1,0:T(8,128)(2,1)}, bf16[3,128,768]{2,1,0:T(8,128)(2,1)}) custom-call(bf16[3,128,768]{2,1,0:T(8,128)(2,1)} %inp_ref.1, bf16[3,128,768]{2,1,0:T(8,128)(2,1)} %cot_ref.1, f32[768]{0:T(1024)} %gain_row_ref.1, f32[768]{0:T(1024)} %gain_col_ref.1, bf16[768,768]{1,0:T(8,128)(2,1)} %wrk_ref.1, bf16[768,768]{1,0:T(8,128)(2,1)} %wrq_ref.1, ...), custom_call_target="tpu_custom_call" | custom-call | tf_op jit(solution)/shard_map/layer/pallas_call | solution.py:887
  177.7 0.0 copy-start
  177.7 2.0 %copy.16 = bf16[3,128,768]{2,1,0:T(8,128)(2,1)} copy(bf16[3,128,768]{2,1,0:T(8,128)(2,1)} %get-tuple-element.4) | data formatting | bytes 1179648
  179.6 0.0 copy-done
  179.6 0.8 copy.17
Async XLA Ops:
  177.7 2.0 %copy-start = (bf16[3,128,768]{2,1,0:T(8,128)(2,1)S(1)}, bf16[3,128,768]{2,1,0:T(8,128)(2,1)}, u32[]{:S(2)}) copy-start(bf16[3,128,768]{2,1,0:T(8,128)(2,1)} %get-tuple-element.5) | copy-start | bytes 1769476

commit v6 on v5

--- a/solution.py
+++ b/solution.py
@@ -386,12 +386,12 @@
 
 
 def lanes(ref):
-    return jnp.concatenate([ref[t] for t in range(6)], axis=1)
+    return jnp.concatenate([ref[t, :TOKENS, :] for t in range(6)], axis=1)
 
 
 def put_lanes(ref, values):
     for t in range(6):
-        ref[t] = values[:, t * 128 : (t + 1) * 128]
+        ref[t, :TOKENS, :] = values[:, t * 128 : (t + 1) * 128]
 
 
 WRK, WRQ, WRV, WRO, WCO, WCQ, WCK, WCV = range(8)
@@ -882,7 +882,7 @@
     pieces = pltpu.VMEM((HG, 16, 8, 4 * E3), bf16)
     seq = pltpu.VMEM((2, 16, 24, D), bf16)
     tokens_b, tokens_f = pltpu.VMEM((TOKENS, D), bf16), pltpu.VMEM((TOKENS, D), f32)
-    lane_tiles = pltpu.VMEM((6, TOKENS, 128), f32)
+    lane_tiles = pltpu.VMEM((6, TOKENS + 8, 128), f32)
     three, four, sixteen = DMA((HG, 3)), DMA((HG, 4)), DMA((HG, 16))
     return pl.pallas_call(
         functools.partial(layer_kernel, row_scale, col_scale),

time: 181 us -> 181 us (level)
  no operation moved by 1% of the time
where the time goes in v6:
time: 181 us; the launch traced here: 180 us
  Pallas kernels  177 us (98%)
  local copies, waits for them, and re-layouts  2.8 us (2%)
    pallas_call x1, Pallas kernels, layer_call(): pl.pallas_call(functools.partial(layer_kernel, row_scale, col_scale), out...  177 us

profile of v6, /device:TPU:1, one launch (start us, length us, event | category | flops | bytes accessed | tf_op | source)
XLA Modules:
  0.0 180.5 jit_solution(2478977213989599887)
XLA Ops:
  0.6 177.0 %layer.1 = (bf16[3,128,768]{2,1,0:T(8,128)(2,1)}, bf16[3,128,768]{2,1,0:T(8,128)(2,1)}) custom-call(bf16[3,128,768]{2,1,0:T(8,128)(2,1)} %inp_ref.1, bf16[3,128,768]{2,1,0:T(8,128)(2,1)} %cot_ref.1, f32[768]{0:T(1024)} %gain_row_ref.1, f32[768]{0:T(1024)} %gain_col_ref.1, bf16[768,768]{1,0:T(8,128)(2,1)} %wrk_ref.1, bf16[768,768]{1,0:T(8,128)(2,1)} %wrq_ref.1, ...), custom_call_target="tpu_custom_call" | custom-call | tf_op jit(solution)/shard_map/layer/pallas_call | solution.py:887
  177.7 0.0 copy-start
  177.7 2.0 %copy.16 = bf16[3,128,768]{2,1,0:T(8,128)(2,1)} copy(bf16[3,128,768]{2,1,0:T(8,128)(2,1)} %get-tuple-element.4) | data formatting | bytes 1179648
  179.7 0.0 copy-done
  179.7 0.8 copy.17
Async XLA Ops:
  177.7 2.0 %copy-start = (bf16[3,128,768]{2,1,0:T(8,128)(2,1)S(1)}, bf16[3,128,768]{2,1,0:T(8,128)(2,1)}, u32[]{:S(2)}) copy-start(bf16[3,128,768]{2,1,0:T(8,128)(2,1)} %get-tuple-element.5) | copy-start | bytes 1769476
